TPU v7x, 32 devices: a whole 2x2x4 slice. The times are simulated.
32 devices in a mesh: lon: 8 (over y, x, core), lat: 4 (over z).
Axes of the slice: x: 2, y: 2, z: 4, core: 2. Of those that a mesh axis runs over, the one named last changes fastest.
Arguments:
- temp: float32 [4, 256, 6144], P(None, 'lat', 'lon'), may hold values from -6 to 6
- salt: float32 [4, 256, 6144], P(None, 'lat', 'lon'), may hold values from -6 to 6
- uvel: float32 [4, 256, 6144], P(None, 'lat', 'lon'), may hold values from -6 to 6
- vvel: float32 [4, 256, 6144], P(None, 'lat', 'lon'), may hold values from -6 to 6
- thick: float32 [4, 256, 6144], P(None, 'lat', 'lon'), may hold values from 0.5 to 2
- land: int32 [4, 256, 6144], P(None, 'lat', 'lon'), may hold values 0 or 1
- east_width: float32 [256, 6144], P('lat', 'lon'), may hold values from 0.5 to 2
- north_width: float32 [256, 6144], P('lat', 'lon'), may hold values from 0.5 to 2
- coriolis: float32 [256, 6144], P('lat', 'lon'), may hold values from 0.5 to 1.5
Outputs:
- temp_next: float32 [4, 256, 6144], P(None, 'lat', 'lon')
- salt_next: float32 [4, 256, 6144], P(None, 'lat', 'lon')
- uvel_next: float32 [4, 256, 6144], P(None, 'lat', 'lon')
- vvel_next: float32 [4, 256, 6144], P(None, 'lat', 'lon')
All inputs are finite; a program needn't handle non-finite values. No bound on the sum of `land` on one device may be relied on, other than what follows from the above.
Results may differ from a plain program's by a relative error of at most 0.00002.
Values sent between devices are 32-bit elements; how exact they have to be, the bound alone decides.
A program may use at most 128 MiB of HBM per device.

v0:
```python
import jax
import jax.numpy as jnp
from jax import lax
from jax.sharding import PartitionSpec as P

time_step = 0.2
biharm_coef = 0.02
alpha_temp = 0.2
beta_salt = 0.8
thin_floor = 0.25


def with_halo(cells, sides, width, closed):
    for axis, dim in sides:
        count = lax.axis_size(axis)
        ends = count if closed else count - 1
        head = lax.slice_in_dim(cells, 0, width, axis=dim)
        tail = lax.slice_in_dim(cells, cells.shape[dim] - width, cells.shape[dim], axis=dim)
        cells = jnp.concatenate(
            [
                lax.ppermute(tail, axis, [(i, (i + 1) % count) for i in range(ends)]),
                cells,
                lax.ppermute(head, axis, [((i + 1) % count, i) for i in range(ends)]),
            ],
            axis=dim,
        )
    return cells


def partner(shard, axis, bit):
    return lax.ppermute(shard, axis, [(i, i ^ 1 << bit) for i in range(lax.axis_size(axis))])


def laplace(field, east_coef, north_coef, volume):
    east_diff = east_coef * (field[..., 1:] - field[..., :-1])
    north_diff = north_coef * (field[..., 1:, :] - field[..., :-1, :])
    return (
        east_diff[..., 1:-1, 1:]
        - east_diff[..., 1:-1, :-1]
        + north_diff[..., 1:, 1:-1]
        - north_diff[..., :-1, 1:-1]
    ) / volume


def advance_level(
    fields, depth_ext, east_ext, north_ext, overhead, wet_cells, coriolis, east_width, north_width
):
    lon_thick = jnp.minimum(depth_ext[:, :-1], depth_ext[:, 1:])
    lat_thick = jnp.minimum(depth_ext[:-1], depth_ext[1:])
    east_coef = (
        lon_thick * (north_ext[:, :-1] + north_ext[:, 1:]) / (east_ext[:, :-1] + east_ext[:, 1:])
    )
    north_coef = lat_thick * (east_ext[:-1] + east_ext[1:]) / (north_ext[:-1] + north_ext[1:])
    volume = east_ext * north_ext * jnp.maximum(depth_ext, thin_floor)
    cycle_lap = laplace(fields, east_coef, north_coef, volume[1:-1, 1:-1])
    biharmonic = laplace(
        cycle_lap, east_coef[1:-1, 1:-1], north_coef[1:-1, 1:-1], volume[2:-2, 2:-2]
    )
    transport_east = (
        lon_thick
        * (north_ext[:, :-1] + north_ext[:, 1:])
        * (fields[2][:, :-1] + fields[2][:, 1:])
        / 4.0
    )
    transport_north = (
        lat_thick * (east_ext[:-1] + east_ext[1:]) * (fields[3][:-1] + fields[3][1:]) / 4.0
    )
    tracers = fields[:2]
    flux_east = transport_east * (tracers[..., :-1] + tracers[..., 1:]) / 2.0
    flux_north = transport_north * (tracers[..., :-1, :] + tracers[..., 1:, :]) / 2.0
    advect = (
        flux_east[..., 2:-2, 2:-1]
        - flux_east[..., 2:-2, 1:-2]
        + flux_north[..., 2:-1, 2:-2]
        - flux_north[..., 1:-2, 2:-2]
    ) / volume[2:-2, 2:-2]
    buoyancy = (beta_salt * fields[1] - alpha_temp * fields[0]) * depth_ext
    pressure = overhead + 0.5 * buoyancy
    overhead = overhead + buoyancy
    grad_east = (pressure[2:-2, 3:-1] - pressure[2:-2, 1:-3]) / (2.0 * east_width)
    grad_north = (pressure[3:-1, 2:-2] - pressure[1:-3, 2:-2]) / (2.0 * north_width)
    interior = fields[:, 2:-2, 2:-2]
    temp_out = wet_cells * (interior[0] - time_step * advect[0] - biharm_coef * biharmonic[0])
    salt_out = wet_cells * (interior[1] - time_step * advect[1] - biharm_coef * biharmonic[1])
    uvel_out = wet_cells * (
        interior[2] + time_step * (coriolis * interior[3] - grad_east) - biharm_coef * biharmonic[2]
    )
    vvel_out = wet_cells * (
        interior[3]
        + time_step * (-coriolis * interior[2] - grad_north)
        - biharm_coef * biharmonic[3]
    )
    return ((temp_out, salt_out, uvel_out, vvel_out), overhead)


def lat_rim(stacked):
    return with_halo(stacked, (("lat", 1),), 2, False)


def lon_rim(stacked):
    return with_halo(stacked, (("lon", 2),), 2, True)


def fold_ghost(top_rows, sign_list):
    mirror = top_rows
    for bit_number in range(lax.axis_size("lon").bit_length() - 1):
        mirror = partner(mirror, "lon", bit_number)
    mirror = mirror[..., ::-1]
    mirror = mirror * sign_list[:, None, None]
    return jnp.stack([mirror[:, 1], mirror[:, 0]], axis=1)


def extend_local(stacked, sign_list):
    on_top = lax.axis_index("lat") == lax.axis_size("lat") - 1
    tall_stack = lat_rim(stacked)
    ghost_rows = fold_ghost(stacked[:, -3:, :], sign_list)
    north_rows = jnp.where(on_top, ghost_rows, tall_stack[:, -2:, :])
    tall_stack = jnp.concatenate([tall_stack[:, :-2, :], north_rows], axis=1)
    return lon_rim(tall_stack)


def shards(temp, salt, uvel, vvel, thick, land, east_width, north_width, coriolis):
    level_count = temp.shape[0]
    depth = land.astype(jnp.float32) * thick
    stacked = jnp.concatenate(
        [temp, salt, uvel, vvel, depth, east_width[None], north_width[None]], axis=0
    )
    sign_list = jnp.concatenate(
        [
            jnp.ones((2 * level_count,), jnp.float32),
            -jnp.ones((2 * level_count,), jnp.float32),
            jnp.ones((level_count + 2,), jnp.float32),
        ]
    )
    extended = extend_local(stacked, sign_list)
    row_ids = lax.broadcasted_iota(jnp.int32, extended[0].shape, 0)
    southern = jnp.logical_and(lax.axis_index("lat") == 0, row_ids < 2)
    east_ext = jnp.where(southern, 1.0, extended[5 * level_count])
    north_ext = jnp.where(southern, 1.0, extended[5 * level_count + 1])
    overhead = jnp.zeros_like(east_ext)
    results = []
    for level_index in range(level_count):
        fields = jnp.stack(
            [
                extended[level_index],
                extended[level_count + level_index],
                extended[2 * level_count + level_index],
                extended[3 * level_count + level_index],
            ]
        )
        outputs, overhead = advance_level(
            fields,
            extended[4 * level_count + level_index],
            east_ext,
            north_ext,
            overhead,
            land[level_index].astype(jnp.float32),
            coriolis,
            east_width,
            north_width,
        )
        results.append(outputs)
    return (
        jnp.stack([r[0] for r in results]),
        jnp.stack([r[1] for r in results]),
        jnp.stack([r[2] for r in results]),
        jnp.stack([r[3] for r in results]),
    )


def solution(mesh):
    in_specs = (
        P(None, "lat", "lon"),
        P(None, "lat", "lon"),
        P(None, "lat", "lon"),
        P(None, "lat", "lon"),
        P(None, "lat", "lon"),
        P(None, "lat", "lon"),
        P("lat", "lon"),
        P("lat", "lon"),
        P("lat", "lon"),
    )
    out_specs = (
        P(None, "lat", "lon"),
        P(None, "lat", "lon"),
        P(None, "lat", "lon"),
        P(None, "lat", "lon"),
    )
    return jax.shard_map(shards, mesh=mesh, in_specs=in_specs, out_specs=out_specs, check_vma=False)
```

profile of v0, /device:TPU:0, one launch (start us, length us, event | category | flops | bytes accessed | tf_op | source)
XLA Modules:
  0.0 65.2 jit_solution(14160283173917014713)
XLA Ops:
  0.7 1.3 %constant_dynamic-update-slice_fusion.3 = f32[22,64,768]{2,1,0:T(8,128)S(1)} fusion(f32[4,64,768]{2,1,0:T(8,128)} %param.9), kind=kLoop, calls=%fused_computation.365 | loop fusion | bytes 1572864
  2.0 1.2 %constant_dynamic-update-slice_fusion.2 = f32[22,64,768]{2,1,0:T(8,128)S(1)} fusion(f32[22,64,768]{2,1,0:T(8,128)S(1)} %constant_dynamic-update-slice_fusion.3, f32[4,64,768]{2,1,0:T(8,128)} %param.10), kind=kLoop, calls=%fused_computation.364 | loop fusion | bytes 1572864
  3.3 1.2 %constant_dynamic-update-slice_fusion.1 = f32[22,64,768]{2,1,0:T(8,128)S(1)} fusion(f32[22,64,768]{2,1,0:T(8,128)S(1)} %constant_dynamic-update-slice_fusion.2, f32[4,64,768]{2,1,0:T(8,128)} %param.11), kind=kLoop, calls=%fused_computation.363 | loop fusion | bytes 1572864
  4.8 0.5 collective-permute-start.1
  5.4 1.1 %collective-permute-done.1 = f32[22,3,768]{2,0,1:T(8,128)S(1)} collective-permute-done((f32[22,3,768]{2,0,1:T(8,128)S(1)}, f32[22,3,768]{2,0,1:T(8,128)S(1)}, u32[]{:S(2)}, u32[]{:S(2)}) %collective-permute-start.1) | collective-permute-done | bytes 202784 | tf_op jit(solution)/shard_map/ppermute | solution.py:31
  6.5 2.9 %collective-permute-start.2 = (f32[22,3,768]{2,0,1:T(8,128)S(1)}, f32[22,3,768]{2,0,1:T(8,128)S(1)}, u32[]{:S(2)}, u32[]{:S(2)}) collective-permute-start(f32[22,3,768]{2,0,1:T(8,128)S(1)} %collective-permute-done.1), channel_id=1, source_target_pairs={{0,8},{4,12},{8,0},{12,4},{16,24},{20,28},{24,16},{28,20},{1,9},{5... | collective-permute-start | bytes 608264 | tf_op jit(solution)/shard_map/ppermute | solution.py:31
  9.3 5.7 %collective-permute-done.2 = f32[22,3,768]{2,0,1:T(8,128)S(1)} collective-permute-done((f32[22,3,768]{2,0,1:T(8,128)S(1)}, f32[22,3,768]{2,0,1:T(8,128)S(1)}, u32[]{:S(2)}, u32[]{:S(2)}) %collective-permute-start.2) | collective-permute-done | bytes 202784 | tf_op jit(solution)/shard_map/ppermute | solution.py:31
  15.1 1.8 %collective-permute-start.3 = (f32[22,3,768]{2,0,1:T(8,128)S(1)}, f32[22,3,768]{2,0,1:T(8,128)S(1)}, u32[]{:S(2)}, u32[]{:S(2)}) collective-permute-start(f32[22,3,768]{2,0,1:T(8,128)S(1)} %collective-permute-done.2), channel_id=1, source_target_pairs={{0,16},{4,20},{8,24},{12,28},{16,0},{20,4},{24,8},{28,12},{1,17},{... | collective-permute-start | bytes 608264 | tf_op jit(solution)/shard_map/ppermute | solution.py:31
  16.9 3.5 %collective-permute-start = (f32[22,2,768]{2,1,0:T(2,128)S(1)}, f32[22,2,768]{2,1,0:T(2,128)S(1)}, u32[]{:S(2)}, u32[]{:S(2)}) collective-permute-start(f32[22,2,768]{2,1,0:T(2,128)S(1)} %get-tuple-element.70), channel_id=1, source_target_pairs={{0,1},{1,2},{2,3},{4,5},{5,6},{6,7},{8,9},{9,10},{10,11},{12,13},{... | collective-permute-start | bytes 405512 | tf_op jit(solution)/shard_map/ppermute | solution.py:21
  20.4 1.3 %collective-permute-start.4 = (f32[22,2,768]{2,1,0:T(2,128)S(1)}, f32[22,2,768]{2,1,0:T(2,128)S(1)}, u32[]{:S(2)}, u32[]{:S(2)}) collective-permute-start(f32[22,2,768]{2,1,0:T(2,128)S(1)} %get-tuple-element.71), channel_id=1, source_target_pairs={{1,0},{2,1},{3,2},{5,4},{6,5},{7,6},{9,8},{10,9},{11,10},{13,12},{... | collective-permute-start | bytes 405512 | tf_op jit(solution)/shard_map/ppermute | solution.py:23
  21.7 0.3 collective-permute-done.3
  22.0 0.5 rev.3
  22.8 4.6 %collective-permute-done.4 = f32[22,2,768]{2,1,0:T(2,128)S(1)} collective-permute-done((f32[22,2,768]{2,1,0:T(2,128)S(1)}, f32[22,2,768]{2,1,0:T(2,128)S(1)}, u32[]{:S(2)}, u32[]{:S(2)}) %collective-permute-start.4) | collective-permute-done | bytes 135200 | tf_op jit(solution)/shard_map/ppermute | solution.py:23
  27.5 1.7 %pad_maximum_fusion.7 = (f32[22,68,2]{2,1,0:T(8,128)S(1)}, f32[22,68,2]{2,1,0:T(8,128)S(1)}) fusion(f32[22,2,768]{2,1,0:T(2,128)S(1)} %maximum_select_fusion, f32[22,64,768]{2,1,0:T(8,128)} %copy-done, f32[22,2,768]{2,1,0:T(2,128)S(1)} %collective-permute-done), kind=kLoop, calls=%fused_computation.55 | loop fusion | flops 11968 | bytes 4619648 | tf_op jit(solution)/shard_map/slice | solution.py:18
  29.2 0.3 copy.55
  29.5 0.3 copy.56
  29.9 0.5 collective-permute-start.5
  30.4 3.7 %collective-permute-done.5 = f32[22,68,2]{1,2,0:T(2,128)S(1)} collective-permute-done((f32[22,68,2]{1,2,0:T(2,128)S(1)}, f32[22,68,2]{1,2,0:T(2,128)S(1)}, u32[]{:S(2)}, u32[]{:S(2)}) %collective-permute-start.5) | collective-permute-done | bytes 12000 | tf_op jit(solution)/shard_map/ppermute | solution.py:21
  34.1 0.4 copy.57
  34.5 0.4 copy.58
  34.9 5.5 %pad_maximum_fusion = f32[22,68,772]{2,1,0:T(8,128)S(1)} fusion(f32[22,68,2]{2,1,0:T(8,128)S(1)} %copy.58, f32[22,2,768]{2,1,0:T(2,128)S(1)} %maximum_select_fusion, f32[22,64,768]{2,1,0:T(8,128)} %copy-done, f32[22,2,768]{2,1,0:T(2,128)S(1)} %collective-permute-done, f32[22,68,2]{2,1,0:T(8,128)S(1)} %copy.57), kind=kLoop, calls=%fused_computation | loop fusion | flops 4619648 | bytes 9239296 | tf_op jit(solution)/shard_map/concatenate | solution.py:19
  40.5 0.2 multiply_add_fusion.1
  40.9 0.2 multiply_add_fusion
  41.9 0.3 fusion.198
  42.4 0.3 fusion.82
  42.8 0.3 fusion.95
  43.1 0.4 fusion.188
  43.6 0.2 pad_maximum_fusion.1
  43.8 0.3 fusion.19
  44.4 0.4 fusion.86
  45.1 0.4 fusion.14
  45.9 0.2 pad_maximum_fusion.3
  46.1 0.3 fusion.9
  46.8 0.3 fusion.4
  47.3 1.0 %fusion.17 = f32[4,66,770]{2,1,0:T(8,128)S(1)} fusion(f32[4,67,772]{2,1,0:T(8,128)S(1)} %fusion.18, f32[4,68,771]{2,1,0:T(8,128)S(1)} %fusion.19, f32[66,770]{1,0:T(8,128)S(1)} %slice.1209), kind=kLoop, calls=%fused_computation.42 | loop fusion | flops 813120 | bytes 4268880 | tf_op jit(solution)/shard_map/div | solution.py:37
  48.3 0.3 fusion.16
  48.8 1.0 %fusion.12 = f32[4,66,770]{2,1,0:T(8,128)S(1)} fusion(f32[4,67,772]{2,1,0:T(8,128)S(1)} %fusion.13, f32[4,68,771]{2,1,0:T(8,128)S(1)} %fusion.14, f32[66,770]{1,0:T(8,128)S(1)} %slice.1254), kind=kLoop, calls=%fused_computation.30 | loop fusion | flops 813120 | bytes 4268880 | tf_op jit(solution)/shard_map/div | solution.py:37
  49.8 0.3 fusion.11
  50.3 1.0 %fusion.7 = f32[4,66,770]{2,1,0:T(8,128)S(1)} fusion(f32[4,67,772]{2,1,0:T(8,128)S(1)} %fusion.8, f32[4,68,771]{2,1,0:T(8,128)S(1)} %fusion.9, f32[66,770]{1,0:T(8,128)S(1)} %slice.1299), kind=kLoop, calls=%fused_computation.18 | loop fusion | flops 813120 | bytes 4268880 | tf_op jit(solution)/shard_map/div | solution.py:37
  51.2 0.3 fusion.6
  51.7 1.0 %fusion.2 = f32[4,66,770]{2,1,0:T(8,128)S(1)} fusion(f32[4,67,772]{2,1,0:T(8,128)S(1)} %fusion.3, f32[4,68,771]{2,1,0:T(8,128)S(1)} %fusion.4, f32[66,770]{1,0:T(8,128)S(1)} %slice.1344), kind=kLoop, calls=%fused_computation.6 | loop fusion | flops 813120 | bytes 4268880 | tf_op jit(solution)/shard_map/div | solution.py:37
  52.7 0.3 fusion.1
  53.2 0.6 fusion.49
  53.8 0.2 fusion.45
  54.0 0.2 fusion.27
  54.2 0.5 fusion.63
  54.7 0.7 %fusion.23 = f32[4,64,768]{2,1,0:T(8,128)S(1)} fusion(f32[4,65,770]{2,1,0:T(8,128)S(1)} %fusion.15, f32[4,66,769]{2,1,0:T(8,128)S(1)} %fusion.16, f32[64,768]{1,0:T(8,128)S(1)} %slice.1193), kind=kLoop, calls=%fused_computation.69 | loop fusion | flops 786432 | bytes 4128768 | tf_op jit(solution)/shard_map/div | solution.py:37
  55.5 0.5 fusion.62
  56.0 0.7 %fusion.22 = f32[4,64,768]{2,1,0:T(8,128)S(1)} fusion(f32[4,65,770]{2,1,0:T(8,128)S(1)} %fusion.10, f32[4,66,769]{2,1,0:T(8,128)S(1)} %fusion.11, f32[64,768]{1,0:T(8,128)S(1)} %slice.1242), kind=kLoop, calls=%fused_computation.65 | loop fusion | flops 786432 | bytes 4128768 | tf_op jit(solution)/shard_map/div | solution.py:37
  56.7 0.3 fusion.127
  57.1 0.4 fusion.119
  57.5 0.2 fusion.171
  57.7 0.4 fusion.31
  58.0 0.5 fusion.61
  58.5 0.7 %fusion.21 = f32[4,64,768]{2,1,0:T(8,128)S(1)} fusion(f32[4,65,770]{2,1,0:T(8,128)S(1)} %fusion.5, f32[4,66,769]{2,1,0:T(8,128)S(1)} %fusion.6, f32[64,768]{1,0:T(8,128)S(1)} %slice.1287), kind=kLoop, calls=%fused_computation.61 | loop fusion | flops 786432 | bytes 4128768 | tf_op jit(solution)/shard_map/div | solution.py:37
  59.3 0.4 fusion.111
  59.6 0.5 fusion.60
  60.1 0.7 %fusion.20 = f32[4,64,768]{2,1,0:T(8,128)S(1)} fusion(f32[4,65,770]{2,1,0:T(8,128)S(1)} %fusion, f32[4,66,769]{2,1,0:T(8,128)S(1)} %fusion.1, f32[64,768]{1,0:T(8,128)S(1)} %slice.1332), kind=kLoop, calls=%fused_computation.57 | loop fusion | flops 786432 | bytes 4128768 | tf_op jit(solution)/shard_map/div | solution.py:37
  60.8 0.3 fusion.103
  61.2 0.2 fusion.165
  61.4 0.9 %pad_maximum_fusion.11 = f32[4,64,768]{2,1,0:T(8,128)} fusion(f32[1,64,768]{2,1,0:T(8,128)S(1)} %get-tuple-element.78, f32[1,64,768]{2,1,0:T(8,128)S(1)} %get-tuple-element.76, f32[1,64,768]{2,1,0:T(8,128)S(1)} %get-tuple-element.74, f32[1,64,768]{2,1,0:T(8,128)S(1)} %get-tuple-element.72), kind=kLoop, calls=%fused_computation.75 | loop fusion | flops 589824 | bytes 1572864 | tf_op jit(solution)/shard_map/stack | solution.py:167
  62.3 0.9 %pad_maximum_fusion.9 = f32[4,64,768]{2,1,0:T(8,128)} fusion(f32[1,64,768]{2,1,0:T(8,128)S(1)} %get-tuple-element.88, f32[1,64,768]{2,1,0:T(8,128)S(1)} %get-tuple-element.91, f32[1,64,768]{2,1,0:T(8,128)S(1)} %get-tuple-element.82, f32[1,64,768]{2,1,0:T(8,128)S(1)} %get-tuple-element.85), kind=kLoop, calls=%fused_computation.73 | loop fusion | flops 589824 | bytes 1572864 | tf_op jit(solution)/shard_map/stack | solution.py:165
  63.3 0.9 %pad_maximum_fusion.10 = f32[4,64,768]{2,1,0:T(8,128)} fusion(f32[1,64,768]{2,1,0:T(8,128)S(1)} %get-tuple-element.79, f32[1,64,768]{2,1,0:T(8,128)S(1)} %get-tuple-element.77, f32[1,64,768]{2,1,0:T(8,128)S(1)} %get-tuple-element.75, f32[1,64,768]{2,1,0:T(8,128)S(1)} %get-tuple-element.73), kind=kLoop, calls=%fused_computation.74 | loop fusion | flops 589824 | bytes 1572864 | tf_op jit(solution)/shard_map/stack | solution.py:166
  64.2 0.9 %pad_maximum_fusion.8 = f32[4,64,768]{2,1,0:T(8,128)} fusion(f32[1,64,768]{2,1,0:T(8,128)S(1)} %get-tuple-element.89, f32[1,64,768]{2,1,0:T(8,128)S(1)} %get-tuple-element.90, f32[1,64,768]{2,1,0:T(8,128)S(1)} %get-tuple-element.83, f32[1,64,768]{2,1,0:T(8,128)S(1)} %get-tuple-element.84), kind=kLoop, calls=%fused_computation.72 | loop fusion | flops 589824 | bytes 1572864 | tf_op jit(solution)/shard_map/stack | solution.py:164
  (68 shorter events, 4.5 us)
Async XLA Ops:
  0.6 3.8 %copy-start.7 = (f32[4,64,768]{2,1,0:T(8,128)S(1)}, f32[4,64,768]{2,1,0:T(8,128)}, u32[]{:S(2)}) copy-start(f32[4,64,768]{2,1,0:T(8,128)} %param.12) | copy-start | bytes 2359300
  0.6 3.9 %copy-start.1 = (s32[4,64,768]{2,1,0:T(8,128)S(1)}, s32[4,64,768]{2,1,0:T(8,128)}, u32[]{:S(2)}) copy-start(s32[4,64,768]{2,1,0:T(8,128)} %param.14) | copy-start | bytes 2359300
  0.7 3.9 %copy-start.10 = (f32[4,64,768]{2,1,0:T(8,128)S(1)}, f32[4,64,768]{2,1,0:T(8,128)}, u32[]{:S(2)}) copy-start(f32[4,64,768]{2,1,0:T(8,128)} %param.13) | copy-start | bytes 2359300
  0.7 4.0 %copy-start.2 = (f32[64,768]{1,0:T(8,128)S(1)}, f32[64,768]{1,0:T(8,128)}, u32[]{:S(2)}) copy-start(f32[64,768]{1,0:T(8,128)} %param.15) | copy-start | bytes 589828
  0.7 4.0 %copy-start.3 = (f32[64,768]{1,0:T(8,128)S(1)}, f32[64,768]{1,0:T(8,128)}, u32[]{:S(2)}) copy-start(f32[64,768]{1,0:T(8,128)} %param.16) | copy-start | bytes 589828
  3.2 19.2 %copy-start.11 = (f32[22]{0:T(128)S(1)}, f32[22]{0:T(128)}, u32[]{:S(2)}) copy-start(f32[22]{0:T(128)} %constant.38.clone.1) | copy-start | bytes 268
  4.7 12.1 %copy-start = (f32[22,64,768]{2,1,0:T(8,128)}, f32[22,64,768]{2,1,0:T(8,128)S(1)}, u32[]{:S(2)}) copy-start(f32[22,64,768]{2,1,0:T(8,128)S(1)} %bitcast_dynamic-update-slice_fusion) | copy-start | bytes 12976132
  4.8 1.6 %collective-permute-start.1 = (f32[22,3,768]{2,0,1:T(8,128)S(1)}, f32[22,3,768]{2,0,1:T(8,128)S(1)}, u32[]{:S(2)}, u32[]{:S(2)}) collective-permute-start(f32[22,3,768]{2,0,1:T(8,128)S(1)} %copy.52), channel_id=1, source_target_pairs={{0,4},{4,0},{8,12},{12,8},{16,20},{20,16},{24,28},{28,24},{1,5},{5... | collective-permute-start | bytes 608264 | tf_op jit(solution)/shard_map/ppermute | solution.py:31
  6.5 8.6 %collective-permute-start.2 = (f32[22,3,768]{2,0,1:T(8,128)S(1)}, f32[22,3,768]{2,0,1:T(8,128)S(1)}, u32[]{:S(2)}, u32[]{:S(2)}) collective-permute-start(f32[22,3,768]{2,0,1:T(8,128)S(1)} %collective-permute-done.1), channel_id=1, source_target_pairs={{0,8},{4,12},{8,0},{12,4},{16,24},{20,28},{24,16},{28,20},{1,9},{5... | collective-permute-start | bytes 608264 | tf_op jit(solution)/shard_map/ppermute | solution.py:31
  15.1 7.0 %collective-permute-start.3 = (f32[22,3,768]{2,0,1:T(8,128)S(1)}, f32[22,3,768]{2,0,1:T(8,128)S(1)}, u32[]{:S(2)}, u32[]{:S(2)}) collective-permute-start(f32[22,3,768]{2,0,1:T(8,128)S(1)} %collective-permute-done.2), channel_id=1, source_target_pairs={{0,16},{4,20},{8,24},{12,28},{16,0},{20,4},{24,8},{28,12},{1,17},{... | collective-permute-start | bytes 608264 | tf_op jit(solution)/shard_map/ppermute | solution.py:31
  16.9 10.6 %collective-permute-start = (f32[22,2,768]{2,1,0:T(2,128)S(1)}, f32[22,2,768]{2,1,0:T(2,128)S(1)}, u32[]{:S(2)}, u32[]{:S(2)}) collective-permute-start(f32[22,2,768]{2,1,0:T(2,128)S(1)} %get-tuple-element.70), channel_id=1, source_target_pairs={{0,1},{1,2},{2,3},{4,5},{5,6},{6,7},{8,9},{9,10},{10,11},{12,13},{... | collective-permute-start | bytes 405512 | tf_op jit(solution)/shard_map/ppermute | solution.py:21
  20.4 6.9 %collective-permute-start.4 = (f32[22,2,768]{2,1,0:T(2,128)S(1)}, f32[22,2,768]{2,1,0:T(2,128)S(1)}, u32[]{:S(2)}, u32[]{:S(2)}) collective-permute-start(f32[22,2,768]{2,1,0:T(2,128)S(1)} %get-tuple-element.71), channel_id=1, source_target_pairs={{1,0},{2,1},{3,2},{5,4},{6,5},{7,6},{9,8},{10,9},{11,10},{13,12},{... | collective-permute-start | bytes 405512 | tf_op jit(solution)/shard_map/ppermute | solution.py:23
  29.8 4.6 %collective-permute-start.6 = (f32[22,68,2]{1,2,0:T(2,128)S(1)}, f32[22,68,2]{1,2,0:T(2,128)S(1)}, u32[]{:S(2)}, u32[]{:S(2)}) collective-permute-start(f32[22,68,2]{1,2,0:T(2,128)S(1)} %copy.56), channel_id=1, source_target_pairs={{4,0},{8,4},{12,8},{16,12},{20,16},{24,20},{28,24},{0,28},{5,1},{9... | collective-permute-start | bytes 35912 | tf_op jit(solution)/shard_map/ppermute | solution.py:23
  29.9 4.2 %collective-permute-start.5 = (f32[22,68,2]{1,2,0:T(2,128)S(1)}, f32[22,68,2]{1,2,0:T(2,128)S(1)}, u32[]{:S(2)}, u32[]{:S(2)}) collective-permute-start(f32[22,68,2]{1,2,0:T(2,128)S(1)} %copy.55), channel_id=1, source_target_pairs={{0,4},{4,8},{8,12},{12,16},{16,20},{20,24},{24,28},{28,0},{1,5},{5... | collective-permute-start | bytes 35912 | tf_op jit(solution)/shard_map/ppermute | solution.py:21
  54.7 2.0 %copy-start.6 = (f32[4,64,768]{2,1,0:T(8,128)S(1)}, f32[4,64,768]{2,1,0:T(8,128)}, u32[]{:S(2)}) copy-start(f32[4,64,768]{2,1,0:T(8,128)} %param.11) | copy-start | bytes 2359300
  54.7 2.0 %copy-start.8 = (f32[4,64,768]{2,1,0:T(8,128)S(1)}, f32[4,64,768]{2,1,0:T(8,128)}, u32[]{:S(2)}) copy-start(f32[4,64,768]{2,1,0:T(8,128)} %param.12) | copy-start | bytes 2359300
  54.7 2.0 %copy-start.9 = (f32[64,768]{1,0:T(8,128)S(1)}, f32[64,768]{1,0:T(8,128)}, u32[]{:S(2)}) copy-start(f32[64,768]{1,0:T(8,128)} %param.17) | copy-start | bytes 589828
  55.9 1.5 %copy-start.4 = (f32[4,64,768]{2,1,0:T(8,128)S(1)}, f32[4,64,768]{2,1,0:T(8,128)}, u32[]{:S(2)}) copy-start(f32[4,64,768]{2,1,0:T(8,128)} %param.9) | copy-start | bytes 2359300
  56.0 1.5 %copy-start.5 = (f32[4,64,768]{2,1,0:T(8,128)S(1)}, f32[4,64,768]{2,1,0:T(8,128)}, u32[]{:S(2)}) copy-start(f32[4,64,768]{2,1,0:T(8,128)} %param.10) | copy-start | bytes 2359300
where the time goes:
time: 65.4 us; the launch traced here: 65.2 us
  other arithmetic  29.4 us (45%)
  waiting for transfers between devices  15.4 us (24%)
  starting transfers between devices  10.5 us (16%)
  local copies, waits for them, and re-layouts  8.58 us (13%)
  between operations  1.36 us (2%)
    ppermute x3, waiting for transfers between devices, partner(): lax.ppermute(shard, axis, [(i, i ^ 1 << bit) for i in range(lax.axis_size...  7.11 us
    div x8, other arithmetic, laplace(): (east_diff[..., 1:-1, 1:] - east_diff[..., 1:-1, :-1] + north_diff[..., 1...  6.82 us
    concatenate x1, other arithmetic, with_halo(): jnp.concatenate([lax.ppermute(tail, axis, [(i, (i + 1) % count) for i in...  5.46 us
    ppermute x3, starting transfers between devices, partner(): lax.ppermute(shard, axis, [(i, i ^ 1 << bit) for i in range(lax.axis_size...  5.15 us
    ppermute x2, waiting for transfers between devices, with_halo(): lax.ppermute(head, axis, [((i + 1) % count, i) for i in range(ends)])  4.56 us
    ppermute x2, starting transfers between devices, with_halo(): lax.ppermute(tail, axis, [(i, (i + 1) % count) for i in range(ends)])  3.99 us
    unnamed x29, local copies, waits for them, and re-layouts  3.87 us
    ppermute x2, waiting for transfers between devices, with_halo(): lax.ppermute(tail, axis, [(i, (i + 1) % count) for i in range(ends)])  3.68 us
  transfers between devices with their start and end apart: 7, of which 5 were waited for; matrix products, arithmetic and copies ran while one was open for 2% of the time, Pallas kernels for 0%

commit v1 on v0

v1 whole, which is shorter than its diff:
```python
import functools

import jax
import jax.numpy as jnp
from jax import lax
from jax.experimental import pallas as pl
from jax.experimental.pallas import tpu as pltpu
from jax.sharding import PartitionSpec as P

time_step = 0.2
biharm_coef = 0.02
alpha_temp = 0.2
beta_salt = 0.8
thin_floor = 0.25

LANES = 128
PAD = 8


def kernel(
    n_lat, n_lon,
    temp, salt, uvel, vvel, thick, land, east_width, north_width, coriolis,
    temp_out, salt_out, uvel_out, vvel_out,
    q, th, la, cor, lap, cf, pres, base, ob,
    row_pack, row_recv, col_pack, corner_pack, col_recv,
    in_sem, out_sem, row_send, row_sem, col_send, col_sem, corner_send,
):
    levels, rows, width = temp.shape
    nc = width // LANES
    nb = rows // 8
    nf = 5 * levels + 2
    fa, fb = 5 * levels, 5 * levels + 1
    lat, lon = lax.axis_index("lat"), lax.axis_index("lon")
    top = lat == n_lat - 1
    south = lat > 0
    east_lon = lax.rem(lon + 1, n_lon)
    west_lon = lax.rem(lon + n_lon - 1, n_lon)
    lat_n = jnp.where(top, lat, lat + 1)
    lat_s = jnp.where(south, lat - 1, 0)
    north = (lat_n, jnp.where(top, n_lon - 1 - lon, lon))
    fold_e = lax.rem(2 * n_lon - 2 - lon, n_lon)
    fold_w = lax.rem(n_lon - lon, n_lon)
    north_e = (lat_n, jnp.where(top, fold_e, east_lon))
    north_w = (lat_n, jnp.where(top, fold_w, west_lon))
    e_self = jnp.logical_and(top, fold_e == lon)
    w_self = jnp.logical_and(top, fold_w == lon)
    e_far, w_far = jnp.logical_not(e_self), jnp.logical_not(w_self)
    east, west = (lat, east_lon), (lat, west_lon)

    barrier = pltpu.get_barrier_semaphore()

    def greet(where):
        pl.semaphore_signal(barrier, inc=1, device_id={"lat": where[0], "lon": where[1]}, device_id_type=pl.DeviceIdType.MESH)

    greet(east)
    greet(west)
    greet(north)

    @pl.when(e_far)
    def _():
        greet(north_e)

    @pl.when(w_far)
    def _():
        greet(north_w)

    @pl.when(south)
    def _():
        greet((lat_s, lon))
        greet((lat_s, east_lon))
        greet((lat_s, west_lon))

    order = [0, nc - 1] + list(range(1, nc - 1))
    loads = {}
    sem_at = 0
    for c in order:
        cols = pl.ds(c * LANES, LANES)
        here = []
        for src, dst in (
            (land, la.at[:, c]),
            (thick, th.at[:, c]),
            (temp, q.at[0:levels, c, PAD:PAD + rows]),
            (salt, q.at[levels:2 * levels, c, PAD:PAD + rows]),
            (uvel, q.at[2 * levels:3 * levels, c, PAD:PAD + rows]),
            (vvel, q.at[3 * levels:4 * levels, c, PAD:PAD + rows]),
        ):
            here.append(pltpu.make_async_copy(src.at[:, :, cols], dst, in_sem.at[sem_at]))
            sem_at += 1
        for src, dst in (
            (east_width, q.at[fa, c, PAD:PAD + rows]),
            (north_width, q.at[fb, c, PAD:PAD + rows]),
            (coriolis, cor.at[c]),
        ):
            here.append(pltpu.make_async_copy(src.at[:, cols], dst, in_sem.at[sem_at]))
            sem_at += 1
        for copy in here:
            copy.start()
        loads[c] = here

    lane = lax.broadcasted_iota(jnp.int32, (8, LANES), 1)
    sub = lax.broadcasted_iota(jnp.int32, (8, LANES), 0)
    first, last = lane == 0, lane == LANES - 1

    def finish_load(c):
        for copy in loads[c]:
            copy.wait()
        for l in range(levels):
            q[4 * levels + l, c, PAD:PAD + rows, :] = la[l, c].astype(jnp.float32) * th[l, c]

    finish_load(0)
    finish_load(nc - 1)
    lane_r = lax.broadcasted_iota(jnp.int32, (rows, LANES), 1)
    head = jnp.zeros((rows, LANES), jnp.float32)
    tail = jnp.zeros((rows, LANES), jnp.float32)
    for f in range(nf):
        mine = lane_r // 2 == f
        a0 = q[f, 0, PAD:PAD + rows, :]
        a1 = q[f, nc - 1, PAD:PAD + rows, :]
        head = jnp.where(mine, pltpu.roll(a0, 2 * f, 1) if f else a0, head)
        tail = jnp.where(mine, pltpu.roll(a1, 2 * f + 2, 1), tail)
    col_pack[0] = head.reshape(nb, 8, LANES)
    col_pack[1] = tail.reshape(nb, 8, LANES)
    sign_lane = jnp.where(
        jnp.logical_and(lane >= 4 * levels, lane < 8 * levels), -1.0, 1.0
    ).astype(jnp.float32)
    for side, block in ((0, head), (1, tail)):
        x = block[rows - 8:rows, :]
        y = jnp.where(lane % 2 == 0, pltpu.roll(x, LANES - 1, 1), pltpu.roll(x, 1, 1)) * sign_lane
        y = jnp.where(sub == 0, pltpu.roll(y, 2, 0), pltpu.roll(y, 4, 0))
        corner_pack[side] = jnp.where(top, y, x)

    partners = 3 + e_far.astype(jnp.int32) + w_far.astype(jnp.int32) + 3 * south.astype(jnp.int32)
    pl.semaphore_wait(barrier, partners)

    def send(src, dst, s_sem, r_sem, where):
        return pltpu.make_async_remote_copy(
            src_ref=src, dst_ref=dst, send_sem=s_sem, recv_sem=r_sem,
            device_id={"lat": where[0], "lon": where[1]}, device_id_type=pl.DeviceIdType.MESH,
        )

    to_east = send(col_pack.at[1], col_recv.at[1, 1:nb + 1], col_send.at[1], col_sem.at[1, 1], east)
    to_west = send(col_pack.at[0], col_recv.at[0, 1:nb + 1], col_send.at[0], col_sem.at[0, 1], west)
    e_side = jnp.where(top, 0, 1)
    w_side = jnp.where(top, 1, 0)
    blk = jnp.where(top, nb + 1, 0)
    which = jnp.where(top, 2, 0)
    to_ne = send(corner_pack.at[1], col_recv.at[e_side, blk], corner_send.at[0], col_sem.at[e_side, which], north_e)
    to_nw = send(corner_pack.at[0], col_recv.at[w_side, blk], corner_send.at[1], col_sem.at[w_side, which], north_w)
    to_se = send(col_pack.at[1, 0], col_recv.at[1, nb + 1], corner_send.at[2], col_sem.at[1, 2], (lat_s, east_lon))
    to_sw = send(col_pack.at[0, 0], col_recv.at[0, nb + 1], corner_send.at[3], col_sem.at[0, 2], (lat_s, west_lon))
    to_east.start()
    to_west.start()

    for c in range(1, nc - 1):
        finish_load(c)
    flip = jnp.where(top, -1.0, 1.0).astype(jnp.float32)
    for f in range(nf):
        row_pack[0, :, 2 * f:2 * f + 2, :] = q[f, 0:nc, PAD:PAD + 2, :]
        s0 = PAD + rows - 2
        near = q[f, 0:nc, s0:s0 + 1, :]
        far = jnp.where(top, q[f, 0:nc, s0 - 1:s0, :], q[f, 0:nc, s0 + 1:s0 + 2, :])
        if 2 * levels <= f < 4 * levels:
            near, far = near * flip, far * flip
        row_pack[1, :, 2 * f:2 * f + 1, :] = near
        row_pack[1, :, 2 * f + 1:2 * f + 2, :] = far

    @pl.when(top)
    def _():
        i0 = lax.broadcasted_iota(jnp.int32, (LANES, LANES), 0)
        i1 = lax.broadcasted_iota(jnp.int32, (LANES, LANES), 1)
        mirror = (i0 + i1 == LANES - 1).astype(jnp.float32)
        turned = [
            jnp.dot(row_pack[1, c, 0:2 * nf, :], mirror, precision=lax.Precision.HIGHEST,
                    preferred_element_type=jnp.float32)
            for c in range(nc)
        ]
        for c in range(nc):
            row_pack[1, nc - 1 - c, 0:2 * nf, :] = turned[c]

    slot = jnp.where(top, 1, 0)
    to_north = send(row_pack.at[1], row_recv.at[slot], row_send.at[1], row_sem.at[slot], north)
    to_south = send(row_pack.at[0], row_recv.at[1], row_send.at[0], row_sem.at[1], (lat_s, lon))
    to_north.start()

    @pl.when(south)
    def _():
        to_south.start()
        to_se.start()
        to_sw.start()

    @pl.when(e_far)
    def _():
        to_ne.start()

    @pl.when(w_far)
    def _():
        to_nw.start()

    ring = nc + 1

    def to_e(x, beside):
        return pltpu.roll(jnp.where(first, beside, x), LANES - 1, 1)

    def to_w(x, beside):
        return pltpu.roll(jnp.where(last, beside, x), 1, 1)

    def pass_a(s, c):
        cp, cm = lax.rem(c + 1, ring), lax.rem(c + ring - 1, ring)
        r0, rn, rs = pl.ds(s, 8), pl.ds(s + 1, 8), pl.ds(s - 1, 8)

        def five(f):
            x = q[f, c, r0, :]
            return (x, to_e(x, q[f, cp, r0, :]), to_w(x, q[f, cm, r0, :]), q[f, c, rn, :], q[f, c, rs, :])

        a, ae, aw, an, as_ = five(fa)
        b, be, bw, bn, bs = five(fb)
        iarea = 1.0 / (a * b)
        we, ww, wn, ws = b + be, b + bw, a + an, a + as_
        re, rw, rn_, rs_ = we / (a + ae), ww / (a + aw), wn / (b + bn), ws / (b + bs)
        k = time_step / 8.0
        we, ww, wn, ws = we * k, ww * k, wn * k, ws * k
        over = jnp.zeros_like(a)
        for l in range(levels):
            d, de, dw, dn, ds_ = five(4 * levels + l)
            inv = iarea / jnp.maximum(d, thin_floor)
            me = jnp.minimum(d, de) * inv
            mw = jnp.minimum(d, dw) * inv
            mn = jnp.minimum(d, dn) * inv
            ms = jnp.minimum(d, ds_) * inv
            ce, cw, cn, cs = me * re, mw * rw, mn * rn_, ms * rs_
            cf[l, c, r0, :] = ce
            cf[levels + l, c, r0, :] = cw
            cf[2 * levels + l, c, r0, :] = cn
            cf[3 * levels + l, c, r0, :] = cs

            def laplace(v, x, xe, xw, xn, xs):
                lap[v * levels + l, c, r0, :] = (
                    ce * (xe - x) + cw * (xw - x) + cn * (xn - x) + cs * (xs - x)
                )

            u = five(2 * levels + l)
            laplace(2, *u)
            te = me * we * (u[0] + u[1])
            tw = mw * ww * (u[0] + u[2])
            v = five(3 * levels + l)
            laplace(3, *v)
            tn = mn * wn * (v[0] + v[3])
            ts = ms * ws * (v[0] + v[4])
            tracer = []
            for i in range(2):
                x, xe, xw, xn, xs = five(i * levels + l)
                laplace(i, x, xe, xw, xn, xs)
                advect = te * (x + xe) - tw * (x + xw) + tn * (x + xn) - ts * (x + xs)
                base[i * levels + l, c, r0, :] = x - advect
                tracer.append(x)
            buoyancy = (beta_salt * tracer[1] - alpha_temp * tracer[0]) * d
            pres[l, c, r0, :] = over + 0.5 * buoyancy
            over = over + buoyancy

    def pass_b(j, c):
        cp, cm = lax.rem(c + 1, ring), lax.rem(c + ring - 1, ring)
        s = pl.multiple_of(PAD + 8 * j, 8)
        t = pl.multiple_of(8 * j, 8)
        r0, rn, rs, ro = pl.ds(s, 8), pl.ds(s + 1, 8), pl.ds(s - 1, 8), pl.ds(t, 8)
        ga = (0.5 * time_step) / q[fa, c, r0, :]
        gb = (0.5 * time_step) / q[fb, c, r0, :]
        rot = time_step * cor[c, ro, :]
        for l in range(levels):
            ce, cw = cf[l, c, r0, :], cf[levels + l, c, r0, :]
            cn, cs = cf[2 * levels + l, c, r0, :], cf[3 * levels + l, c, r0, :]
            wet = la[l, c, ro, :].astype(jnp.float32)

            def drag(v):
                f = v * levels + l
                x = lap[f, c, r0, :]
                xe, xw = to_e(x, lap[f, cp, r0, :]), to_w(x, lap[f, cm, r0, :])
                xn, xs = lap[f, c, rn, :], lap[f, c, rs, :]
                return biharm_coef * (
                    ce * (xe - x) + cw * (xw - x) + cn * (xn - x) + cs * (xs - x)
                )

            for i in range(2):
                ob[i * levels + l, c, ro, :] = wet * (base[i * levels + l, c, r0, :] - drag(i))
            p = pres[l, c, r0, :]
            ge = (to_e(p, pres[l, cp, r0, :]) - to_w(p, pres[l, cm, r0, :])) * ga
            gn = (pres[l, c, rn, :] - pres[l, c, rs, :]) * gb
            u, v = q[2 * levels + l, c, r0, :], q[3 * levels + l, c, r0, :]
            ob[2 * levels + l, c, ro, :] = wet * (u + (rot * v - ge) - drag(2))
            ob[3 * levels + l, c, ro, :] = wet * (v - (rot * u + gn) - drag(3))

    def loop(count, body):
        lax.fori_loop(0, count, lambda i, carry: (body(i), carry)[1], 0)

    def unpack_cols(block):
        s = pl.multiple_of(8 * block, 8)
        e, w = col_recv[0, block], col_recv[1, block]
        for f in range(nf):
            x = pltpu.roll(e, LANES - 2 * f, 1) if f else e
            q[f, nc, pl.ds(s, 8), :] = jnp.where(lane < 64, x, pltpu.roll(w, LANES - 2 - 2 * f, 1))

    inner = nc - 2
    loop((nb - 1) * inner, lambda i: pass_a(PAD - 1 + 8 * (1 + i // inner), 1 + lax.rem(i, inner)))
    to_east.wait_recv()
    to_west.wait_recv()
    loop(nb, lambda i: unpack_cols(i + 1))
    loop(
        (nb - 1) * 3,
        lambda i: pass_a(PAD - 1 + 8 * (1 + i // 3), lax.rem(nc - 1 + lax.rem(i, 3), ring)),
    )
    loop((nb - 2) * nc, lambda i: pass_b(1 + i // nc, lax.rem(i, nc)))

    outs = (temp_out, salt_out, uvel_out, vvel_out)
    stores = []

    def store(part, lo, size):
        for i, dst in enumerate(outs):
            for c in range(nc):
                copy = pltpu.make_async_copy(
                    ob.at[i * levels:(i + 1) * levels, c, lo:lo + size],
                    dst.at[:, lo:lo + size, c * LANES:(c + 1) * LANES],
                    out_sem.at[part, i * nc + c],
                )
                copy.start()
                stores.append(copy)

    store(0, 8, rows - 16)

    @pl.when(south)
    def _():
        send(row_pack.at[1], row_recv.at[0], row_send.at[1], row_sem.at[0], north).wait_recv()
        send(corner_pack.at[1], col_recv.at[1, 0], corner_send.at[0], col_sem.at[1, 0], east).wait_recv()
        send(corner_pack.at[0], col_recv.at[0, 0], corner_send.at[1], col_sem.at[0, 0], west).wait_recv()
        for f in range(nf):
            q[f, 0:nc, PAD - 2:PAD, :] = row_recv[0, :, 2 * f:2 * f + 2, :]
        unpack_cols(0)

    @pl.when(jnp.logical_not(south))
    def _():
        for f in range(nf):
            q[f, :, 0:PAD, :] = jnp.full((ring, PAD, LANES), 1.0 if f >= fa else 0.0, jnp.float32)

    send(row_pack.at[0], row_recv.at[1], row_send.at[0], row_sem.at[1], north).wait_recv()

    @pl.when(e_far)
    def _():
        send(corner_pack.at[1], col_recv.at[0, nb + 1], corner_send.at[0], col_sem.at[0, 2], east).wait_recv()

    @pl.when(e_self)
    def _():
        col_recv[0, nb + 1] = corner_pack[1]

    @pl.when(w_far)
    def _():
        send(corner_pack.at[0], col_recv.at[1, nb + 1], corner_send.at[1], col_sem.at[1, 2], west).wait_recv()

    @pl.when(w_self)
    def _():
        col_recv[1, nb + 1] = corner_pack[0]

    for f in range(nf):
        q[f, 0:nc, PAD + rows:PAD + rows + 2, :] = row_recv[1, :, 2 * f:2 * f + 2, :]
    unpack_cols(nb + 1)

    loop(2 * ring, lambda i: pass_a(PAD - 1 + (rows - 6) * (i // ring), lax.rem(i, ring)))
    loop(2 * nc, lambda i: pass_b((nb - 1) * (i // nc), lax.rem(i, nc)))
    store(1, 0, 8)
    store(2, rows - 8, 8)

    to_east.wait_send()
    to_west.wait_send()
    to_north.wait_send()

    @pl.when(south)
    def _():
        to_south.wait_send()
        to_se.wait_send()
        to_sw.wait_send()

    @pl.when(e_far)
    def _():
        to_ne.wait_send()

    @pl.when(w_far)
    def _():
        to_nw.wait_send()

    for copy in stores:
        copy.wait()


def shards(n_lat, n_lon, *args):
    levels, rows, width = args[0].shape
    nc, nb, nf = width // LANES, rows // 8, 5 * levels + 2
    tall = rows + 2 * PAD
    row_slots = -(-2 * nf // 8) * 8
    f32 = jnp.float32

    def plane(count):
        return pltpu.VMEM((count, nc + 1, tall, LANES), f32)

    dma = pltpu.SemaphoreType.DMA
    return pl.pallas_call(
        functools.partial(kernel, n_lat, n_lon),
        out_shape=tuple(jax.ShapeDtypeStruct((levels, rows, width), f32) for _ in range(4)),
        in_specs=[pl.BlockSpec(memory_space=pl.ANY)] * 9,
        out_specs=tuple(pl.BlockSpec(memory_space=pl.ANY) for _ in range(4)),
        scratch_shapes=[
            plane(nf),
            pltpu.VMEM((levels, nc, rows, LANES), f32),
            pltpu.VMEM((levels, nc, rows, LANES), jnp.int32),
            pltpu.VMEM((nc, rows, LANES), f32),
            plane(4 * levels),
            plane(4 * levels),
            plane(levels),
            plane(2 * levels),
            pltpu.VMEM((4 * levels, nc, rows, LANES), f32),
            pltpu.VMEM((2, nc, row_slots, LANES), f32),
            pltpu.VMEM((2, nc, row_slots, LANES), f32),
            pltpu.VMEM((2, nb, 8, LANES), f32),
            pltpu.VMEM((2, 8, LANES), f32),
            pltpu.VMEM((2, nb + 2, 8, LANES), f32),
            dma((9 * nc,)),
            dma((3, 4 * nc)),
            dma((2,)),
            dma((2,)),
            dma((2,)),
            dma((2, 3)),
            dma((4,)),
        ],
        compiler_params=pltpu.CompilerParams(
            collective_id=0, has_side_effects=True, vmem_limit_bytes=40 * 1024 * 1024
        ),
    )(*args)


def solution(mesh):
    grid, line = P(None, "lat", "lon"), P("lat", "lon")
    body = functools.partial(shards, mesh.shape["lat"], mesh.shape["lon"])
    return jax.shard_map(
        body, mesh=mesh, in_specs=(grid,) * 6 + (line,) * 3, out_specs=(grid,) * 4, check_vma=False
    )
```

time: 65.4 us -> 37.7 us (0.58)
  other arithmetic: 29.4 us -> 0 us
  Pallas kernels: 0 us -> 23.5 us
  waiting for transfers between devices: 15.4 us -> 0 us
  starting transfers between devices: 10.5 us -> 0 us
  local copies, waits for them, and re-layouts: 8.58 us -> 13.1 us
  between operations: 1.36 us -> 0.66 us
    pallas_call x0 -> x1, Pallas kernels: none -> 23.5 us  [shards(): pl.pallas_call(functools.partial(kernel, n_lat, n_lon), out_shape=tuple((...]
    ppermute x7 -> x0, waiting for transfers between devices: 15.4 us -> none  [the longest x3 7.11 us: partner(): lax.ppermute(shard, axis, [(i, i ^ 1 << bit) for i in range(lax.axis_size...]
    div x22 -> x0, other arithmetic: 11.7 us -> none  [the longest x8 6.82 us: laplace(): (east_diff[..., 1:-1, 1:] - east_diff[..., 1:-1, :-1] + north_diff[..., 1...]
    ppermute x7 -> x0, starting transfers between devices: 10.5 us -> none  [the longest x3 5.15 us: partner(): lax.ppermute(shard, axis, [(i, i ^ 1 << bit) for i in range(lax.axis_size...]
    unnamed x29 -> x22, local copies, waits for them, and re-layouts: 3.87 us -> 13.1 us
    another operation x10 -> x0, other arithmetic: 5.46 us -> none  [the longest x5 2.33 us: shards(): jnp.stack([r[3] for r in results])]
    concatenate x1 -> x0, other arithmetic: 5.46 us -> none  [with_halo(): jnp.concatenate([lax.ppermute(tail, axis, [(i, (i + 1) % count) for i in...]
    mul x20 -> x0, other arithmetic: 4.47 us -> none  [the longest x8 2.74 us: laplace(): east_diff = east_coef * (field[..., 1:] - field[..., :-1])]
  transfers between devices with their start and end apart: 7 -> 0, of which waited for: 5 -> 0; matrix products, arithmetic and copies ran while one was open for 2% -> 0% of each run, Pallas kernels for 0% -> 0%
where the time goes in v1:
time: 37.7 us; the launch traced here: 37.3 us
  Pallas kernels  23.5 us (62%)
  local copies, waits for them, and re-layouts  13.1 us (35%)
  between operations  0.66 us (2%)
    pallas_call x1, Pallas kernels, shards(): pl.pallas_call(functools.partial(kernel, n_lat, n_lon), out_shape=tuple((...  23.5 us
    unnamed x22, local copies, waits for them, and re-layouts  13.1 us

profile of v1, /device:TPU:0, one launch (start us, length us, event | category | flops | bytes accessed | tf_op | source)
XLA Modules:
  0.0 37.3 jit_solution(3622409610955943581)
XLA Ops:
  0.6 0.0 copy-start
  0.6 1.1 %copy-done = f32[4,64,768]{2,1,0:T(8,128)S(1)} copy-done((f32[4,64,768]{2,1,0:T(8,128)S(1)}, f32[4,64,768]{2,1,0:T(8,128)}, u32[]{:S(2)}) %copy-start) | copy-done | bytes 786456
  1.8 0.0 copy-start.1
  1.8 1.1 %copy-done.1 = f32[4,64,768]{2,1,0:T(8,128)S(1)} copy-done((f32[4,64,768]{2,1,0:T(8,128)S(1)}, f32[4,64,768]{2,1,0:T(8,128)}, u32[]{:S(2)}) %copy-start.1) | copy-done | bytes 786456
  2.9 0.0 copy-start.2
  2.9 1.1 %copy-done.2 = f32[4,64,768]{2,1,0:T(8,128)S(1)} copy-done((f32[4,64,768]{2,1,0:T(8,128)S(1)}, f32[4,64,768]{2,1,0:T(8,128)}, u32[]{:S(2)}) %copy-start.2) | copy-done | bytes 786456
  4.0 0.0 copy-start.3
  4.0 1.1 %copy-done.3 = f32[4,64,768]{2,1,0:T(8,128)S(1)} copy-done((f32[4,64,768]{2,1,0:T(8,128)S(1)}, f32[4,64,768]{2,1,0:T(8,128)}, u32[]{:S(2)}) %copy-start.3) | copy-done | bytes 786456
  5.2 0.0 copy-start.4
  5.2 1.1 %copy-done.4 = f32[4,64,768]{2,1,0:T(8,128)S(1)} copy-done((f32[4,64,768]{2,1,0:T(8,128)S(1)}, f32[4,64,768]{2,1,0:T(8,128)}, u32[]{:S(2)}) %copy-start.4) | copy-done | bytes 786456
  6.3 0.0 copy-start.5
  6.3 1.1 %copy-done.5 = s32[4,64,768]{2,1,0:T(8,128)S(1)} copy-done((s32[4,64,768]{2,1,0:T(8,128)S(1)}, s32[4,64,768]{2,1,0:T(8,128)}, u32[]{:S(2)}) %copy-start.5) | copy-done | bytes 786456
  7.4 0.0 copy-start.6
  7.4 0.9 %copy-done.6 = f32[64,768]{1,0:T(8,128)S(1)} copy-done((f32[64,768]{1,0:T(8,128)S(1)}, f32[64,768]{1,0:T(8,128)}, u32[]{:S(2)}) %copy-start.6) | copy-done | bytes 196632
  8.4 0.0 copy-start.7
  8.4 0.9 %copy-done.7 = f32[64,768]{1,0:T(8,128)S(1)} copy-done((f32[64,768]{1,0:T(8,128)S(1)}, f32[64,768]{1,0:T(8,128)}, u32[]{:S(2)}) %copy-start.7) | copy-done | bytes 196632
  9.3 0.0 copy-start.8
  9.3 0.9 %copy-done.8 = f32[64,768]{1,0:T(8,128)S(1)} copy-done((f32[64,768]{1,0:T(8,128)S(1)}, f32[64,768]{1,0:T(8,128)}, u32[]{:S(2)}) %copy-start.8) | copy-done | bytes 196632
  10.2 23.5 %shard_map.120 = (f32[4,64,768]{2,1,0:T(8,128)S(1)}, f32[4,64,768]{2,1,0:T(8,128)S(1)}, f32[4,64,768]{2,1,0:T(8,128)S(1)}, f32[4,64,768]{2,1,0:T(8,128)S(1)}) custom-call(f32[4,64,768]{2,1,0:T(8,128)S(1)} %copy-done, f32[4,64,768]{2,1,0:T(8,128)S(1)} %copy-done.1, f32[4,64,768]{2,1,0:T(8,128)S(1)} %copy-done.2, f32[4,64,768]{2,1,0:T(8,128)S(1)} %copy-done.3, ...), custom_call_target="tpu_custom_call" | custom-call | tf_op jit(solution)/shard_map/pallas_call | solution.py:402
  33.8 0.9 %copy.17 = f32[4,64,768]{2,1,0:T(8,128)} copy(f32[4,64,768]{2,1,0:T(8,128)S(1)} %get-tuple-element.8) | data formatting | bytes 1572864
  34.6 0.9 %copy.18 = f32[4,64,768]{2,1,0:T(8,128)} copy(f32[4,64,768]{2,1,0:T(8,128)S(1)} %get-tuple-element.9) | data formatting | bytes 1572864
  35.5 0.9 %copy.19 = f32[4,64,768]{2,1,0:T(8,128)} copy(f32[4,64,768]{2,1,0:T(8,128)S(1)} %get-tuple-element.10) | data formatting | bytes 1572864
  36.4 0.9 %copy.20 = f32[4,64,768]{2,1,0:T(8,128)} copy(f32[4,64,768]{2,1,0:T(8,128)S(1)} %get-tuple-element.11) | data formatting | bytes 1572864
Async XLA Ops:
  0.6 1.1 %copy-start = (f32[4,64,768]{2,1,0:T(8,128)S(1)}, f32[4,64,768]{2,1,0:T(8,128)}, u32[]{:S(2)}) copy-start(f32[4,64,768]{2,1,0:T(8,128)} %temp.1) | copy-start | bytes 2359300
  1.8 1.1 %copy-start.1 = (f32[4,64,768]{2,1,0:T(8,128)S(1)}, f32[4,64,768]{2,1,0:T(8,128)}, u32[]{:S(2)}) copy-start(f32[4,64,768]{2,1,0:T(8,128)} %salt.1) | copy-start | bytes 2359300
  2.9 1.1 %copy-start.2 = (f32[4,64,768]{2,1,0:T(8,128)S(1)}, f32[4,64,768]{2,1,0:T(8,128)}, u32[]{:S(2)}) copy-start(f32[4,64,768]{2,1,0:T(8,128)} %uvel.1) | copy-start | bytes 2359300
  4.0 1.1 %copy-start.3 = (f32[4,64,768]{2,1,0:T(8,128)S(1)}, f32[4,64,768]{2,1,0:T(8,128)}, u32[]{:S(2)}) copy-start(f32[4,64,768]{2,1,0:T(8,128)} %vvel.1) | copy-start | bytes 2359300
  5.2 1.1 %copy-start.4 = (f32[4,64,768]{2,1,0:T(8,128)S(1)}, f32[4,64,768]{2,1,0:T(8,128)}, u32[]{:S(2)}) copy-start(f32[4,64,768]{2,1,0:T(8,128)} %thick.1) | copy-start | bytes 2359300
  6.3 1.1 %copy-start.5 = (s32[4,64,768]{2,1,0:T(8,128)S(1)}, s32[4,64,768]{2,1,0:T(8,128)}, u32[]{:S(2)}) copy-start(s32[4,64,768]{2,1,0:T(8,128)} %land.1) | copy-start | bytes 2359300
  7.4 0.9 %copy-start.6 = (f32[64,768]{1,0:T(8,128)S(1)}, f32[64,768]{1,0:T(8,128)}, u32[]{:S(2)}) copy-start(f32[64,768]{1,0:T(8,128)} %east_width.1) | copy-start | bytes 589828
  8.4 0.9 %copy-start.7 = (f32[64,768]{1,0:T(8,128)S(1)}, f32[64,768]{1,0:T(8,128)}, u32[]{:S(2)}) copy-start(f32[64,768]{1,0:T(8,128)} %north_width.1) | copy-start | bytes 589828
  9.3 0.9 %copy-start.8 = (f32[64,768]{1,0:T(8,128)S(1)}, f32[64,768]{1,0:T(8,128)}, u32[]{:S(2)}) copy-start(f32[64,768]{1,0:T(8,128)} %coriolis.1) | copy-start | bytes 589828

commit v2 on v1

--- a/solution.py
+++ b/solution.py
@@ -14,16 +14,39 @@
 thin_floor = 0.25
 
 LANES = 128
+LIMIT = 32
 PAD = 8
 
 
-def kernel(
+def inverse(x):
+    r = pl.reciprocal(x, approx=True)
+    r = r * (2.0 - x * r)
+    return r * (2.0 - x * r)
+
+
+def loop(count, body):
+    lax.fori_loop(0, count, lambda i, carry: (body(i), carry)[1], 0)
+
+
+def edge_lanes():
+    lane = lax.broadcasted_iota(jnp.int32, (8, LANES), 1)
+    first, last = lane == 0, lane == LANES - 1
+
+    def to_e(x, beside):
+        return pltpu.roll(jnp.where(first, beside, x), LANES - 1, 1)
+
+    def to_w(x, beside):
+        return pltpu.roll(jnp.where(last, beside, x), 1, 1)
+
+    return lane, to_e, to_w
+
+
+def first_kernel(
     n_lat, n_lon,
-    temp, salt, uvel, vvel, thick, land, east_width, north_width, coriolis,
-    temp_out, salt_out, uvel_out, vvel_out,
-    q, th, la, cor, lap, cf, pres, base, ob,
-    row_pack, row_recv, col_pack, corner_pack, col_recv,
-    in_sem, out_sem, row_send, row_sem, col_send, col_sem, corner_send,
+    temp, salt, uvel, vvel, thick, land, east_width, north_width,
+    q, la, lap, cf, pres, base,
+    th, row_pack, row_recv, col_pack, corner_pack, col_recv,
+    in_sem, row_send, row_sem, col_send, col_sem, corner_send,
 ):
     levels, rows, width = temp.shape
     nc = width // LANES
@@ -89,7 +112,6 @@
         for src, dst in (
             (east_width, q.at[fa, c, PAD:PAD + rows]),
             (north_width, q.at[fb, c, PAD:PAD + rows]),
-            (coriolis, cor.at[c]),
         ):
             here.append(pltpu.make_async_copy(src.at[:, cols], dst, in_sem.at[sem_at]))
             sem_at += 1
@@ -97,9 +119,8 @@
             copy.start()
         loads[c] = here
 
-    lane = lax.broadcasted_iota(jnp.int32, (8, LANES), 1)
+    lane, to_e, to_w = edge_lanes()
     sub = lax.broadcasted_iota(jnp.int32, (8, LANES), 0)
-    first, last = lane == 0, lane == LANES - 1
 
     def finish_load(c):
         for copy in loads[c]:
@@ -198,14 +219,8 @@
 
     ring = nc + 1
 
-    def to_e(x, beside):
-        return pltpu.roll(jnp.where(first, beside, x), LANES - 1, 1)
-
-    def to_w(x, beside):
-        return pltpu.roll(jnp.where(last, beside, x), 1, 1)
-
     def pass_a(s, c):
-        cp, cm = lax.rem(c + 1, ring), lax.rem(c + ring - 1, ring)
+        cp, cm = (c + 1) % ring, (c - 1) % ring
         r0, rn, rs = pl.ds(s, 8), pl.ds(s + 1, 8), pl.ds(s - 1, 8)
 
         def five(f):
@@ -214,15 +229,16 @@
 
         a, ae, aw, an, as_ = five(fa)
         b, be, bw, bn, bs = five(fb)
-        iarea = 1.0 / (a * b)
+        iarea = inverse(a * b)
         we, ww, wn, ws = b + be, b + bw, a + an, a + as_
-        re, rw, rn_, rs_ = we / (a + ae), ww / (a + aw), wn / (b + bn), ws / (b + bs)
+        re, rw = we * inverse(a + ae), ww * inverse(a + aw)
+        rn_, rs_ = wn * inverse(b + bn), ws * inverse(b + bs)
         k = time_step / 8.0
         we, ww, wn, ws = we * k, ww * k, wn * k, ws * k
         over = jnp.zeros_like(a)
         for l in range(levels):
             d, de, dw, dn, ds_ = five(4 * levels + l)
-            inv = iarea / jnp.maximum(d, thin_floor)
+            inv = iarea * inverse(jnp.maximum(d, thin_floor))
             me = jnp.minimum(d, de) * inv
             mw = jnp.minimum(d, dw) * inv
             mn = jnp.minimum(d, dn) * inv
@@ -257,13 +273,119 @@
             pres[l, c, r0, :] = over + 0.5 * buoyancy
             over = over + buoyancy
 
+    def unpack_cols(block):
+        s = pl.multiple_of(8 * block, 8)
+        e, w = col_recv[0, block], col_recv[1, block]
+        for f in range(nf):
+            x = pltpu.roll(e, LANES - 2 * f, 1) if f else e
+            q[f, nc, pl.ds(s, 8), :] = jnp.where(lane < 64, x, pltpu.roll(w, LANES - 2 - 2 * f, 1))
+
+    def row_a(s, tiles):
+        for c in tiles:
+            pass_a(s, c)
+
+    def unpack_cols(block):
+        s = pl.multiple_of(8 * block, 8)
+        e, w = col_recv[0, block], col_recv[1, block]
+        for f in range(nf):
+            x = pltpu.roll(e, LANES - 2 * f, 1) if f else e
+            q[f, nc, pl.ds(s, 8), :] = jnp.where(lane < 64, x, pltpu.roll(w, LANES - 2 - 2 * f, 1))
+
+    def row_a(s, tiles):
+        for c in tiles:
+            pass_a(s, c)
+
+    def row_b(j):
+        for c in range(nc):
+            pass_b(j, c)
+
+    loop(nb - 1, lambda k: row_a(PAD - 1 + 8 * (1 + k), range(1, nc - 1)))
+    to_east.wait_recv()
+    to_west.wait_recv()
+    loop(nb, lambda i: unpack_cols(i + 1))
+    loop(nb - 1, lambda k: row_a(PAD - 1 + 8 * (1 + k), (nc - 1, nc, 0)))
+
+    @pl.when(south)
+    def _():
+        send(row_pack.at[1], row_recv.at[0], row_send.at[1], row_sem.at[0], north).wait_recv()
+        send(corner_pack.at[1], col_recv.at[1, 0], corner_send.at[0], col_sem.at[1, 0], east).wait_recv()
+        send(corner_pack.at[0], col_recv.at[0, 0], corner_send.at[1], col_sem.at[0, 0], west).wait_recv()
+        for f in range(nf):
+            q[f, 0:nc, PAD - 2:PAD, :] = row_recv[0, :, 2 * f:2 * f + 2, :]
+        unpack_cols(0)
+
+    @pl.when(jnp.logical_not(south))
+    def _():
+        for f in range(nf):
+            q[f, :, 0:PAD, :] = jnp.full((ring, PAD, LANES), 1.0 if f >= fa else 0.0, jnp.float32)
+
+    send(row_pack.at[0], row_recv.at[1], row_send.at[0], row_sem.at[1], north).wait_recv()
+
+    @pl.when(e_far)
+    def _():
+        send(corner_pack.at[1], col_recv.at[0, nb + 1], corner_send.at[0], col_sem.at[0, 2], east).wait_recv()
+
+    @pl.when(e_self)
+    def _():
+        col_recv[0, nb + 1] = corner_pack[1]
+
+    @pl.when(w_far)
+    def _():
+        send(corner_pack.at[0], col_recv.at[1, nb + 1], corner_send.at[1], col_sem.at[1, 2], west).wait_recv()
+
+    @pl.when(w_self)
+    def _():
+        col_recv[1, nb + 1] = corner_pack[0]
+
+    for f in range(nf):
+        q[f, 0:nc, PAD + rows:PAD + rows + 2, :] = row_recv[1, :, 2 * f:2 * f + 2, :]
+    unpack_cols(nb + 1)
+
+    loop(2, lambda i: row_a(PAD - 1 + (rows - 6) * i, range(ring)))
+
+    to_east.wait_send()
+    to_west.wait_send()
+    to_north.wait_send()
+
+    @pl.when(south)
+    def _():
+        to_south.wait_send()
+        to_se.wait_send()
+        to_sw.wait_send()
+
+    @pl.when(e_far)
+    def _():
+        to_ne.wait_send()
+
+    @pl.when(w_far)
+    def _():
+        to_nw.wait_send()
+
+
+def second_kernel(
+    coriolis, q, la, lap, cf, pres, base, temp_out, salt_out, uvel_out, vvel_out,
+    cor, ob, cor_sem, out_sem,
+):
+    levels, rows, width = temp_out.shape
+    nc, nb = width // LANES, rows // 8
+    fa, fb = 5 * levels, 5 * levels + 1
+    ring = nc + 1
+    loads = []
+    for c in range(nc):
+        copy = pltpu.make_async_copy(
+            coriolis.at[:, c * LANES:(c + 1) * LANES], cor.at[c], cor_sem.at[c]
+        )
+        copy.start()
+        loads.append(copy)
+    lane, to_e, to_w = edge_lanes()
+
     def pass_b(j, c):
-        cp, cm = lax.rem(c + 1, ring), lax.rem(c + ring - 1, ring)
+        cp, cm = (c + 1) % ring, (c - 1) % ring
         s = pl.multiple_of(PAD + 8 * j, 8)
         t = pl.multiple_of(8 * j, 8)
         r0, rn, rs, ro = pl.ds(s, 8), pl.ds(s + 1, 8), pl.ds(s - 1, 8), pl.ds(t, 8)
-        ga = (0.5 * time_step) / q[fa, c, r0, :]
-        gb = (0.5 * time_step) / q[fb, c, r0, :]
+        ga = (0.5 * time_step) * inverse(q[fa, c, r0, :])
+        gb = (0.5 * time_step) * inverse(q[fb, c, r0, :])
         rot = time_step * cor[c, ro, :]
         for l in range(levels):
             ce, cw = cf[l, c, r0, :], cf[levels + l, c, r0, :]
@@ -288,102 +410,27 @@
             ob[2 * levels + l, c, ro, :] = wet * (u + (rot * v - ge) - drag(2))
             ob[3 * levels + l, c, ro, :] = wet * (v - (rot * u + gn) - drag(3))
 
-    def loop(count, body):
-        lax.fori_loop(0, count, lambda i, carry: (body(i), carry)[1], 0)
-
-    def unpack_cols(block):
-        s = pl.multiple_of(8 * block, 8)
-        e, w = col_recv[0, block], col_recv[1, block]
-        for f in range(nf):
-            x = pltpu.roll(e, LANES - 2 * f, 1) if f else e
-            q[f, nc, pl.ds(s, 8), :] = jnp.where(lane < 64, x, pltpu.roll(w, LANES - 2 - 2 * f, 1))
-
-    inner = nc - 2
-    loop((nb - 1) * inner, lambda i: pass_a(PAD - 1 + 8 * (1 + i // inner), 1 + lax.rem(i, inner)))
-    to_east.wait_recv()
-    to_west.wait_recv()
-    loop(nb, lambda i: unpack_cols(i + 1))
-    loop(
-        (nb - 1) * 3,
-        lambda i: pass_a(PAD - 1 + 8 * (1 + i // 3), lax.rem(nc - 1 + lax.rem(i, 3), ring)),
-    )
-    loop((nb - 2) * nc, lambda i: pass_b(1 + i // nc, lax.rem(i, nc)))
-
+    for copy in loads:
+        copy.wait()
     outs = (temp_out, salt_out, uvel_out, vvel_out)
+
+    def row_b(j):
+        for c in range(nc):
+            pass_b(j, c)
+
     stores = []
-
-    def store(part, lo, size):
+    for part in range(2):
+        lo = part * (rows // 2)
+        loop(nb // 2, lambda j: row_b(part * (nb // 2) + j))
         for i, dst in enumerate(outs):
             for c in range(nc):
                 copy = pltpu.make_async_copy(
-                    ob.at[i * levels:(i + 1) * levels, c, lo:lo + size],
-                    dst.at[:, lo:lo + size, c * LANES:(c + 1) * LANES],
+                    ob.at[i * levels:(i + 1) * levels, c, lo:lo + rows // 2],
+                    dst.at[:, lo:lo + rows // 2, c * LANES:(c + 1) * LANES],
                     out_sem.at[part, i * nc + c],
                 )
                 copy.start()
                 stores.append(copy)
-
-    store(0, 8, rows - 16)
-
-    @pl.when(south)
-    def _():
-        send(row_pack.at[1], row_recv.at[0], row_send.at[1], row_sem.at[0], north).wait_recv()
-        send(corner_pack.at[1], col_recv.at[1, 0], corner_send.at[0], col_sem.at[1, 0], east).wait_recv()
-        send(corner_pack.at[0], col_recv.at[0, 0], corner_send.at[1], col_sem.at[0, 0], west).wait_recv()
-        for f in range(nf):
-            q[f, 0:nc, PAD - 2:PAD, :] = row_recv[0, :, 2 * f:2 * f + 2, :]
-        unpack_cols(0)
-
-    @pl.when(jnp.logical_not(south))
-    def _():
-        for f in range(nf):
-            q[f, :, 0:PAD, :] = jnp.full((ring, PAD, LANES), 1.0 if f >= fa else 0.0, jnp.float32)
-
-    send(row_pack.at[0], row_recv.at[1], row_send.at[0], row_sem.at[1], north).wait_recv()
-
-    @pl.when(e_far)
-    def _():
-        send(corner_pack.at[1], col_recv.at[0, nb + 1], corner_send.at[0], col_sem.at[0, 2], east).wait_recv()
-
-    @pl.when(e_self)
-    def _():
-        col_recv[0, nb + 1] = corner_pack[1]
-
-    @pl.when(w_far)
-    def _():
-        send(corner_pack.at[0], col_recv.at[1, nb + 1], corner_send.at[1], col_sem.at[1, 2], west).wait_recv()
-
-    @pl.when(w_self)
-    def _():
-        col_recv[1, nb + 1] = corner_pack[0]
-
-    for f in range(nf):
-        q[f, 0:nc, PAD + rows:PAD + rows + 2, :] = row_recv[1, :, 2 * f:2 * f + 2, :]
-    unpack_cols(nb + 1)
-
-    loop(2 * ring, lambda i: pass_a(PAD - 1 + (rows - 6) * (i // ring), lax.rem(i, ring)))
-    loop(2 * nc, lambda i: pass_b((nb - 1) * (i // nc), lax.rem(i, nc)))
-    store(1, 0, 8)
-    store(2, rows - 8, 8)
-
-    to_east.wait_send()
-    to_west.wait_send()
-    to_north.wait_send()
-
-    @pl.when(south)
-    def _():
-        to_south.wait_send()
-        to_se.wait_send()
-        to_sw.wait_send()
-
-    @pl.when(e_far)
-    def _():
-        to_ne.wait_send()
-
-    @pl.when(w_far)
-    def _():
-        to_nw.wait_send()
-
     for copy in stores:
         copy.wait()
 
@@ -399,28 +446,29 @@
         return pltpu.VMEM((count, nc + 1, tall, LANES), f32)
 
     dma = pltpu.SemaphoreType.DMA
-    return pl.pallas_call(
-        functools.partial(kernel, n_lat, n_lon),
-        out_shape=tuple(jax.ShapeDtypeStruct((levels, rows, width), f32) for _ in range(4)),
-        in_specs=[pl.BlockSpec(memory_space=pl.ANY)] * 9,
-        out_specs=tuple(pl.BlockSpec(memory_space=pl.ANY) for _ in range(4)),
-        scratch_shapes=[
+    held = pl.BlockSpec(memory_space=pltpu.VMEM)
+    far = pl.BlockSpec(memory_space=pl.ANY)
+    args = [pltpu.with_memory_space_constraint(x, pltpu.HBM) for x in args]
+    middle = pl.pallas_call(
+        functools.partial(first_kernel, n_lat, n_lon),
+        out_shape=(
             plane(nf),
-            pltpu.VMEM((levels, nc, rows, LANES), f32),
             pltpu.VMEM((levels, nc, rows, LANES), jnp.int32),
-            pltpu.VMEM((nc, rows, LANES), f32),
             plane(4 * levels),
             plane(4 * levels),
             plane(levels),
             plane(2 * levels),
-            pltpu.VMEM((4 * levels, nc, rows, LANES), f32),
+        ),
+        in_specs=[far] * 8,
+        out_specs=(held,) * 6,
+        scratch_shapes=[
+            pltpu.VMEM((levels, nc, rows, LANES), f32),
             pltpu.VMEM((2, nc, row_slots, LANES), f32),
             pltpu.VMEM((2, nc, row_slots, LANES), f32),
             pltpu.VMEM((2, nb, 8, LANES), f32),
             pltpu.VMEM((2, 8, LANES), f32),
             pltpu.VMEM((2, nb + 2, 8, LANES), f32),
-            dma((9 * nc,)),
-            dma((3, 4 * nc)),
+            dma((8 * nc,)),
             dma((2,)),
             dma((2,)),
             dma((2,)),
@@ -428,9 +476,22 @@
             dma((4,)),
         ],
         compiler_params=pltpu.CompilerParams(
-            collective_id=0, has_side_effects=True, vmem_limit_bytes=40 * 1024 * 1024
+            collective_id=0, has_side_effects=True, vmem_limit_bytes=LIMIT * 1024 * 1024
         ),
-    )(*args)
+    )(*args[:8])
+    return pl.pallas_call(
+        second_kernel,
+        out_shape=tuple(jax.ShapeDtypeStruct((levels, rows, width), f32) for _ in range(4)),
+        in_specs=[far] + [held] * 6,
+        out_specs=(far,) * 4,
+        scratch_shapes=[
+            pltpu.VMEM((nc, rows, LANES), f32),
+            pltpu.VMEM((4 * levels, nc, rows, LANES), f32),
+            dma((nc,)),
+            dma((2, 4 * nc)),
+        ],
+        compiler_params=pltpu.CompilerParams(vmem_limit_bytes=LIMIT * 1024 * 1024),
+    )(args[8], *middle)
 
 
 def solution(mesh):

time: 37.7 us -> 19.3 us (0.51)
  local copies, waits for them, and re-layouts: 13.1 us -> 0 us
  Pallas kernels: 23.5 us -> 18.4 us
    unnamed x22 -> x0, local copies, waits for them, and re-layouts: 13.1 us -> none
    pallas_call x1 -> x2, Pallas kernels: 23.5 us -> 18.4 us  [the longest x1 12.8 us: shards(): pl.pallas_call(functools.partial(first_kernel, n_lat, n_lon), out_shape=(...]
where the time goes in v2:
time: 19.3 us; the launch traced here: 19.1 us
  Pallas kernels  18.4 us (95%)
  between operations  0.64 us (3%)
    pallas_call x1, Pallas kernels, shards(): pl.pallas_call(functools.partial(first_kernel, n_lat, n_lon), out_shape=(...  12.8 us
    pallas_call x1, Pallas kernels, shards(): pl.pallas_call(second_kernel, out_shape=tuple((jax.ShapeDtypeStruct((leve...  5.6 us

profile of v2, /device:TPU:0, one launch (start us, length us, event | category | flops | bytes accessed | tf_op | source)
XLA Modules:
  0.0 19.1 jit_solution(14859818203083916196)
XLA Ops:
  0.6 12.8 %shard_map.120 = (f32[22,7,80,128]{3,2,1,0:T(8,128)S(1)}, s32[4,6,64,128]{3,2,1,0:T(8,128)S(1)}, f32[16,7,80,128]{3,2,1,0:T(8,128)S(1)}, f32[16,7,80,128]{3,2,1,...) custom-call(f32[4,64,768]{2,1,0:T(8,128)} %temp.1, f32[4,64,768]{2,1,0:T(8,128)} %salt.1, ...), custom_call_target="tpu_custom_call" | custom-call | tf_op jit(solution)/shard_map/pallas_call | solution.py:452
  13.5 5.6 %shard_map.121 = (f32[4,64,768]{2,1,0:T(8,128)}, f32[4,64,768]{2,1,0:T(8,128)}, f32[4,64,768]{2,1,0:T(8,128)}, f32[4,64,768]{2,1,0:T(8,128)}) custom-call(f32[64,768]{1,0:T(8,128)} %coriolis.1, f32[22,7,80,128]{3,2,1,0:T(8,128)S(1)} %get-tuple-element.10.q, s32[4,6,64,128]{3,2,1,0:T(8,128)S(1)} %get-tuple-element.11.la, ...), custom_call_target="tpu_custom_call" | custom-call | tf_op jit(solution)/shard_map/pallas_call | solution.py:482

commit v3 on v2

--- a/solution.py
+++ b/solution.py
@@ -15,13 +15,12 @@
 
 LANES = 128
 LIMIT = 32
+PARTS = 4
 PAD = 8
 
 
 def inverse(x):
-    r = pl.reciprocal(x, approx=True)
-    r = r * (2.0 - x * r)
-    return r * (2.0 - x * r)
+    return pl.reciprocal(x, approx=True)
 
 
 def loop(count, body):
@@ -43,10 +42,10 @@
 
 def first_kernel(
     n_lat, n_lon,
-    temp, salt, uvel, vvel, thick, land, east_width, north_width,
-    q, la, lap, cf, pres, base,
-    th, row_pack, row_recv, col_pack, corner_pack, col_recv,
-    in_sem, row_send, row_sem, col_send, col_sem, corner_send,
+    temp, salt, uvel, vvel, thick, land, east_width, north_width, coriolis,
+    q, la, cor, lap, cf, pres, base,
+    th, edge, edge_land, row_pack, row_recv, col_pack, corner_pack, col_recv,
+    edge_sem, in_sem, row_send, row_sem, col_send, col_sem, corner_send,
 ):
     levels, rows, width = temp.shape
     nc = width // LANES
@@ -93,6 +92,22 @@
         greet((lat_s, east_lon))
         greet((lat_s, west_lon))
 
+    edge_loads = []
+    for side, lo in ((0, 0), (1, rows - 8)):
+        for i, (src, dst) in enumerate((
+            (land, edge_land.at[side]),
+            (thick, edge.at[side, 4 * levels:5 * levels]),
+            (temp, edge.at[side, 0:levels]),
+            (salt, edge.at[side, levels:2 * levels]),
+            (uvel, edge.at[side, 2 * levels:3 * levels]),
+            (vvel, edge.at[side, 3 * levels:4 * levels]),
+            (east_width, edge.at[side, fa]),
+            (north_width, edge.at[side, fb]),
+        )):
+            part = src.at[:, lo:lo + 8] if i < 6 else src.at[lo:lo + 8]
+            copy = pltpu.make_async_copy(part, dst, edge_sem.at[8 * side + i])
+            copy.start()
+            edge_loads.append(copy)
     order = [0, nc - 1] + list(range(1, nc - 1))
     loads = {}
     sem_at = 0
@@ -112,6 +127,7 @@
         for src, dst in (
             (east_width, q.at[fa, c, PAD:PAD + rows]),
             (north_width, q.at[fb, c, PAD:PAD + rows]),
+            (coriolis, cor.at[c]),
         ):
             here.append(pltpu.make_async_copy(src.at[:, cols], dst, in_sem.at[sem_at]))
             sem_at += 1
@@ -127,6 +143,55 @@
             copy.wait()
         for l in range(levels):
             q[4 * levels + l, c, PAD:PAD + rows, :] = la[l, c].astype(jnp.float32) * th[l, c]
+
+    for copy in edge_loads:
+        copy.wait()
+    flip = jnp.where(top, -1.0, 1.0).astype(jnp.float32)
+    for side in range(2):
+        for l in range(levels):
+            f = 4 * levels + l
+            edge[side, f] = edge_land[side, l].astype(jnp.float32) * edge[side, f]
+    for f in range(nf):
+        for c in range(nc):
+            cols = slice(c * LANES, (c + 1) * LANES)
+            row_pack[0, c, 2 * f:2 * f + 2, :] = edge[0, f, 0:2, cols]
+            near = edge[1, f, 6:7, cols]
+            far = jnp.where(top, edge[1, f, 5:6, cols], edge[1, f, 7:8, cols])
+            if 2 * levels <= f < 4 * levels:
+                near, far = near * flip, far * flip
+            row_pack[1, c, 2 * f:2 * f + 1, :] = near
+            row_pack[1, c, 2 * f + 1:2 * f + 2, :] = far
+
+    @pl.when(top)
+    def _():
+        i0 = lax.broadcasted_iota(jnp.int32, (LANES, LANES), 0)
+        i1 = lax.broadcasted_iota(jnp.int32, (LANES, LANES), 1)
+        mirror = (i0 + i1 == LANES - 1).astype(jnp.float32)
+        turned = [
+            jnp.dot(row_pack[1, c, 0:2 * nf, :], mirror, precision=lax.Precision.HIGHEST,
+                    preferred_element_type=jnp.float32)
+            for c in range(nc)
+        ]
+        for c in range(nc):
+            row_pack[1, nc - 1 - c, 0:2 * nf, :] = turned[c]
+
+    partners = 3 + e_far.astype(jnp.int32) + w_far.astype(jnp.int32) + 3 * south.astype(jnp.int32)
+    pl.semaphore_wait(barrier, partners)
+
+    def send(src, dst, s_sem, r_sem, where):
+        return pltpu.make_async_remote_copy(
+            src_ref=src, dst_ref=dst, send_sem=s_sem, recv_sem=r_sem,
+            device_id={"lat": where[0], "lon": where[1]}, device_id_type=pl.DeviceIdType.MESH,
+        )
+
+    slot = jnp.where(top, 1, 0)
+    to_north = send(row_pack.at[1], row_recv.at[slot], row_send.at[1], row_sem.at[slot], north)
+    to_south = send(row_pack.at[0], row_recv.at[1], row_send.at[0], row_sem.at[1], (lat_s, lon))
+    to_north.start()
+
+    @pl.when(south)
+    def _():
+        to_south.start()
 
     finish_load(0)
     finish_load(nc - 1)
@@ -150,15 +215,6 @@
         y = jnp.where(sub == 0, pltpu.roll(y, 2, 0), pltpu.roll(y, 4, 0))
         corner_pack[side] = jnp.where(top, y, x)
 
-    partners = 3 + e_far.astype(jnp.int32) + w_far.astype(jnp.int32) + 3 * south.astype(jnp.int32)
-    pl.semaphore_wait(barrier, partners)
-
-    def send(src, dst, s_sem, r_sem, where):
-        return pltpu.make_async_remote_copy(
-            src_ref=src, dst_ref=dst, send_sem=s_sem, recv_sem=r_sem,
-            device_id={"lat": where[0], "lon": where[1]}, device_id_type=pl.DeviceIdType.MESH,
-        )
-
     to_east = send(col_pack.at[1], col_recv.at[1, 1:nb + 1], col_send.at[1], col_sem.at[1, 1], east)
     to_west = send(col_pack.at[0], col_recv.at[0, 1:nb + 1], col_send.at[0], col_sem.at[0, 1], west)
     e_side = jnp.where(top, 0, 1)
@@ -172,51 +228,21 @@
     to_east.start()
     to_west.start()
 
+    @pl.when(south)
+    def _():
+        to_se.start()
+        to_sw.start()
+
+    @pl.when(e_far)
+    def _():
+        to_ne.start()
+
+    @pl.when(w_far)
+    def _():
+        to_nw.start()
+
     for c in range(1, nc - 1):
         finish_load(c)
-    flip = jnp.where(top, -1.0, 1.0).astype(jnp.float32)
-    for f in range(nf):
-        row_pack[0, :, 2 * f:2 * f + 2, :] = q[f, 0:nc, PAD:PAD + 2, :]
-        s0 = PAD + rows - 2
-        near = q[f, 0:nc, s0:s0 + 1, :]
-        far = jnp.where(top, q[f, 0:nc, s0 - 1:s0, :], q[f, 0:nc, s0 + 1:s0 + 2, :])
-        if 2 * levels <= f < 4 * levels:
-            near, far = near * flip, far * flip
-        row_pack[1, :, 2 * f:2 * f + 1, :] = near
-        row_pack[1, :, 2 * f + 1:2 * f + 2, :] = far
-
-    @pl.when(top)
-    def _():
-        i0 = lax.broadcasted_iota(jnp.int32, (LANES, LANES), 0)
-        i1 = lax.broadcasted_iota(jnp.int32, (LANES, LANES), 1)
-        mirror = (i0 + i1 == LANES - 1).astype(jnp.float32)
-        turned = [
-            jnp.dot(row_pack[1, c, 0:2 * nf, :], mirror, precision=lax.Precision.HIGHEST,
-                    preferred_element_type=jnp.float32)
-            for c in range(nc)
-        ]
-        for c in range(nc):
-            row_pack[1, nc - 1 - c, 0:2 * nf, :] = turned[c]
-
-    slot = jnp.where(top, 1, 0)
-    to_north = send(row_pack.at[1], row_recv.at[slot], row_send.at[1], row_sem.at[slot], north)
-    to_south = send(row_pack.at[0], row_recv.at[1], row_send.at[0], row_sem.at[1], (lat_s, lon))
-    to_north.start()
-
-    @pl.when(south)
-    def _():
-        to_south.start()
-        to_se.start()
-        to_sw.start()
-
-    @pl.when(e_far)
-    def _():
-        to_ne.start()
-
-    @pl.when(w_far)
-    def _():
-        to_nw.start()
-
     ring = nc + 1
 
     def pass_a(s, c):
@@ -229,25 +255,27 @@
 
         a, ae, aw, an, as_ = five(fa)
         b, be, bw, bn, bs = five(fb)
-        iarea = inverse(a * b)
+        area = a * b
+        root = biharm_coef ** 0.5
         we, ww, wn, ws = b + be, b + bw, a + an, a + as_
-        re, rw = we * inverse(a + ae), ww * inverse(a + aw)
-        rn_, rs_ = wn * inverse(b + bn), ws * inverse(b + bs)
+        re, rw = (root * we) * inverse(a + ae), (root * ww) * inverse(a + aw)
+        rn_, rs_ = (root * wn) * inverse(b + bn), (root * ws) * inverse(b + bs)
         k = time_step / 8.0
         we, ww, wn, ws = we * k, ww * k, wn * k, ws * k
         over = jnp.zeros_like(a)
         for l in range(levels):
             d, de, dw, dn, ds_ = five(4 * levels + l)
-            inv = iarea * inverse(jnp.maximum(d, thin_floor))
+            inv = inverse(area * jnp.maximum(d, thin_floor))
             me = jnp.minimum(d, de) * inv
             mw = jnp.minimum(d, dw) * inv
             mn = jnp.minimum(d, dn) * inv
             ms = jnp.minimum(d, ds_) * inv
             ce, cw, cn, cs = me * re, mw * rw, mn * rn_, ms * rs_
-            cf[l, c, r0, :] = ce
-            cf[levels + l, c, r0, :] = cw
-            cf[2 * levels + l, c, r0, :] = cn
-            cf[3 * levels + l, c, r0, :] = cs
+            if c < nc:
+                cf[l, c, r0, :] = ce
+                cf[levels + l, c, r0, :] = cw
+                cf[2 * levels + l, c, r0, :] = cn
+                cf[3 * levels + l, c, r0, :] = cs
 
             def laplace(v, x, xe, xw, xn, xs):
                 lap[v * levels + l, c, r0, :] = (
@@ -266,12 +294,17 @@
             for i in range(2):
                 x, xe, xw, xn, xs = five(i * levels + l)
                 laplace(i, x, xe, xw, xn, xs)
-                advect = te * (x + xe) - tw * (x + xw) + tn * (x + xn) - ts * (x + xs)
-                base[i * levels + l, c, r0, :] = x - advect
+                if c < nc:
+                    advect = te * (x + xe) - tw * (x + xw) + tn * (x + xn) - ts * (x + xs)
+                    base[i * levels + l, c, r0, :] = x - advect
                 tracer.append(x)
             buoyancy = (beta_salt * tracer[1] - alpha_temp * tracer[0]) * d
             pres[l, c, r0, :] = over + 0.5 * buoyancy
             over = over + buoyancy
+
+    def row_a(s, tiles):
+        for c in tiles:
+            pass_a(s, c)
 
     def unpack_cols(block):
         s = pl.multiple_of(8 * block, 8)
@@ -284,17 +317,6 @@
         for c in tiles:
             pass_a(s, c)
 
-    def unpack_cols(block):
-        s = pl.multiple_of(8 * block, 8)
-        e, w = col_recv[0, block], col_recv[1, block]
-        for f in range(nf):
-            x = pltpu.roll(e, LANES - 2 * f, 1) if f else e
-            q[f, nc, pl.ds(s, 8), :] = jnp.where(lane < 64, x, pltpu.roll(w, LANES - 2 - 2 * f, 1))
-
-    def row_a(s, tiles):
-        for c in tiles:
-            pass_a(s, c)
-
     def row_b(j):
         for c in range(nc):
             pass_b(j, c)
@@ -363,20 +385,13 @@
 
 
 def second_kernel(
-    coriolis, q, la, lap, cf, pres, base, temp_out, salt_out, uvel_out, vvel_out,
-    cor, ob, cor_sem, out_sem,
+    q, la, cor, lap, cf, pres, base, temp_out, salt_out, uvel_out, vvel_out,
+    ob, out_sem,
 ):
     levels, rows, width = temp_out.shape
     nc, nb = width // LANES, rows // 8
     fa, fb = 5 * levels, 5 * levels + 1
     ring = nc + 1
-    loads = []
-    for c in range(nc):
-        copy = pltpu.make_async_copy(
-            coriolis.at[:, c * LANES:(c + 1) * LANES], cor.at[c], cor_sem.at[c]
-        )
-        copy.start()
-        loads.append(copy)
     lane, to_e, to_w = edge_lanes()
 
     def pass_b(j, c):
@@ -384,6 +399,7 @@
         s = pl.multiple_of(PAD + 8 * j, 8)
         t = pl.multiple_of(8 * j, 8)
         r0, rn, rs, ro = pl.ds(s, 8), pl.ds(s + 1, 8), pl.ds(s - 1, 8), pl.ds(t, 8)
+        cols = slice(c * LANES, (c + 1) * LANES)
         ga = (0.5 * time_step) * inverse(q[fa, c, r0, :])
         gb = (0.5 * time_step) * inverse(q[fb, c, r0, :])
         rot = time_step * cor[c, ro, :]
@@ -397,21 +413,17 @@
                 x = lap[f, c, r0, :]
                 xe, xw = to_e(x, lap[f, cp, r0, :]), to_w(x, lap[f, cm, r0, :])
                 xn, xs = lap[f, c, rn, :], lap[f, c, rs, :]
-                return biharm_coef * (
-                    ce * (xe - x) + cw * (xw - x) + cn * (xn - x) + cs * (xs - x)
-                )
+                return ce * (xe - x) + cw * (xw - x) + cn * (xn - x) + cs * (xs - x)
 
             for i in range(2):
-                ob[i * levels + l, c, ro, :] = wet * (base[i * levels + l, c, r0, :] - drag(i))
+                ob[i * levels + l, ro, cols] = wet * (base[i * levels + l, c, r0, :] - drag(i))
             p = pres[l, c, r0, :]
             ge = (to_e(p, pres[l, cp, r0, :]) - to_w(p, pres[l, cm, r0, :])) * ga
             gn = (pres[l, c, rn, :] - pres[l, c, rs, :]) * gb
             u, v = q[2 * levels + l, c, r0, :], q[3 * levels + l, c, r0, :]
-            ob[2 * levels + l, c, ro, :] = wet * (u + (rot * v - ge) - drag(2))
-            ob[3 * levels + l, c, ro, :] = wet * (v - (rot * u + gn) - drag(3))
-
-    for copy in loads:
-        copy.wait()
+            ob[2 * levels + l, ro, cols] = wet * (u + (rot * v - ge) - drag(2))
+            ob[3 * levels + l, ro, cols] = wet * (v - (rot * u + gn) - drag(3))
+
     outs = (temp_out, salt_out, uvel_out, vvel_out)
 
     def row_b(j):
@@ -419,18 +431,18 @@
             pass_b(j, c)
 
     stores = []
-    for part in range(2):
-        lo = part * (rows // 2)
-        loop(nb // 2, lambda j: row_b(part * (nb // 2) + j))
+    size = rows // PARTS
+    for part in range(PARTS):
+        lo = part * size
+        loop(size // 8, lambda j: row_b(lo // 8 + j))
         for i, dst in enumerate(outs):
-            for c in range(nc):
-                copy = pltpu.make_async_copy(
-                    ob.at[i * levels:(i + 1) * levels, c, lo:lo + rows // 2],
-                    dst.at[:, lo:lo + rows // 2, c * LANES:(c + 1) * LANES],
-                    out_sem.at[part, i * nc + c],
-                )
-                copy.start()
-                stores.append(copy)
+            copy = pltpu.make_async_copy(
+                ob.at[i * levels:(i + 1) * levels, lo:lo + size],
+                dst.at[:, lo:lo + size],
+                out_sem.at[part, i],
+            )
+            copy.start()
+            stores.append(copy)
     for copy in stores:
         copy.wait()
 
@@ -454,21 +466,25 @@
         out_shape=(
             plane(nf),
             pltpu.VMEM((levels, nc, rows, LANES), jnp.int32),
+            pltpu.VMEM((nc, rows, LANES), f32),
             plane(4 * levels),
             plane(4 * levels),
             plane(levels),
             plane(2 * levels),
         ),
-        in_specs=[far] * 8,
-        out_specs=(held,) * 6,
+        in_specs=[far] * 9,
+        out_specs=(held,) * 7,
         scratch_shapes=[
             pltpu.VMEM((levels, nc, rows, LANES), f32),
+            pltpu.VMEM((2, nf, 8, width), f32),
+            pltpu.VMEM((2, levels, 8, width), jnp.int32),
             pltpu.VMEM((2, nc, row_slots, LANES), f32),
             pltpu.VMEM((2, nc, row_slots, LANES), f32),
             pltpu.VMEM((2, nb, 8, LANES), f32),
             pltpu.VMEM((2, 8, LANES), f32),
             pltpu.VMEM((2, nb + 2, 8, LANES), f32),
-            dma((8 * nc,)),
+            dma((16,)),
+            dma((9 * nc,)),
             dma((2,)),
             dma((2,)),
             dma((2,)),
@@ -478,20 +494,18 @@
         compiler_params=pltpu.CompilerParams(
             collective_id=0, has_side_effects=True, vmem_limit_bytes=LIMIT * 1024 * 1024
         ),
-    )(*args[:8])
+    )(*args)
     return pl.pallas_call(
         second_kernel,
         out_shape=tuple(jax.ShapeDtypeStruct((levels, rows, width), f32) for _ in range(4)),
-        in_specs=[far] + [held] * 6,
+        in_specs=[held] * 7,
         out_specs=(far,) * 4,
         scratch_shapes=[
-            pltpu.VMEM((nc, rows, LANES), f32),
-            pltpu.VMEM((4 * levels, nc, rows, LANES), f32),
-            dma((nc,)),
-            dma((2, 4 * nc)),
+            pltpu.VMEM((4 * levels, rows, width), f32),
+            dma((PARTS, 4)),
         ],
         compiler_params=pltpu.CompilerParams(vmem_limit_bytes=LIMIT * 1024 * 1024),
-    )(args[8], *middle)
+    )(*middle)
 
 
 def solution(mesh):

time: 19.3 us -> 18 us (0.933)
  the two profiles are of different devices: /device:TPU:0 before, /device:TPU:25 now
where the time goes in v3:
time: 18 us; the launch traced here: 17.9 us
  Pallas kernels  17.2 us (96%)
  between operations  0.64 us (4%)
    pallas_call x1, Pallas kernels, shards(): pl.pallas_call(functools.partial(first_kernel, n_lat, n_lon), out_shape=(...  13.1 us
    pallas_call x1, Pallas kernels, shards(): pl.pallas_call(second_kernel, out_shape=tuple((jax.ShapeDtypeStruct((leve...  4.08 us

profile of v3, /device:TPU:25, one launch (start us, length us, event | category | flops | bytes accessed | tf_op | source)
XLA Modules:
  0.0 17.9 jit_solution(71439288890040903)
XLA Ops:
  0.6 13.1 %shard_map.120 = (f32[22,7,80,128]{3,2,1,0:T(8,128)S(1)}, s32[4,6,64,128]{3,2,1,0:T(8,128)S(1)}, f32[6,64,128]{2,1,0:T(8,128)S(1)}, f32[16,7,80,128]{3,2,1,0:T(8...) custom-call(f32[4,64,768]{2,1,0:T(8,128)} %temp.1, ...), custom_call_target="tpu_custom_call" | custom-call | tf_op jit(solution)/shard_map/pallas_call | solution.py:464
  13.8 4.1 %shard_map.121 = (f32[4,64,768]{2,1,0:T(8,128)}, f32[4,64,768]{2,1,0:T(8,128)}, f32[4,64,768]{2,1,0:T(8,128)}, f32[4,64,768]{2,1,0:T(8,128)}) custom-call(f32[22,7,80,128]{3,2,1,0:T(8,128)S(1)} %get-tuple-element.11.q, s32[4,6,64,128]{3,2,1,0:T(8,128)S(1)} %get-tuple-element.12.la, f32[6,64,128]{2,1,0:T(8,128)S(1)} %get-tuple-element.13.cor, ...), custom_call_target="tpu_custom_call" | custom-call | tf_op jit(solution)/shard_map/pallas_call | solution.py:498

commit v4 on v3

--- a/solution.py
+++ b/solution.py
@@ -15,7 +15,6 @@
 
 LANES = 128
 LIMIT = 32
-PARTS = 4
 PAD = 8
 
 
@@ -44,8 +43,8 @@
     n_lat, n_lon,
     temp, salt, uvel, vvel, thick, land, east_width, north_width, coriolis,
     q, la, cor, lap, cf, pres, base,
-    th, edge, edge_land, row_pack, row_recv, col_pack, corner_pack, col_recv,
-    edge_sem, in_sem, row_send, row_sem, col_send, col_sem, corner_send,
+    th, edge, row_pack, row_recv, col_pack, corner_pack, col_recv,
+    whole_sem, edge_sem, in_sem, row_send, row_sem, col_send, col_sem, corner_send,
 ):
     levels, rows, width = temp.shape
     nc = width // LANES
@@ -92,48 +91,39 @@
         greet((lat_s, east_lon))
         greet((lat_s, west_lon))
 
+    def begin(src, dst, sem):
+        copy = pltpu.make_async_copy(src, dst, sem)
+        copy.start()
+        return copy
+
+    whole = [begin(land, la, whole_sem.at[0]), begin(thick, th, whole_sem.at[1])]
+    loads = {}
+
+    def begin_tile(c):
+        cols = pl.ds(c * LANES, LANES)
+        here = []
+        for i, src in enumerate((temp, salt, uvel, vvel)):
+            here.append(begin(
+                src.at[:, :, cols], q.at[i * levels:(i + 1) * levels, c, PAD:PAD + rows],
+                in_sem.at[c, i],
+            ))
+        for i, src in enumerate((east_width, north_width)):
+            here.append(begin(src.at[:, cols], q.at[fa + i, c, PAD:PAD + rows], in_sem.at[c, 4 + i]))
+        loads[c] = here
+
+    begin_tile(0)
+    begin_tile(nc - 1)
     edge_loads = []
     for side, lo in ((0, 0), (1, rows - 8)):
-        for i, (src, dst) in enumerate((
-            (land, edge_land.at[side]),
-            (thick, edge.at[side, 4 * levels:5 * levels]),
-            (temp, edge.at[side, 0:levels]),
-            (salt, edge.at[side, levels:2 * levels]),
-            (uvel, edge.at[side, 2 * levels:3 * levels]),
-            (vvel, edge.at[side, 3 * levels:4 * levels]),
-            (east_width, edge.at[side, fa]),
-            (north_width, edge.at[side, fb]),
-        )):
-            part = src.at[:, lo:lo + 8] if i < 6 else src.at[lo:lo + 8]
-            copy = pltpu.make_async_copy(part, dst, edge_sem.at[8 * side + i])
-            copy.start()
-            edge_loads.append(copy)
-    order = [0, nc - 1] + list(range(1, nc - 1))
-    loads = {}
-    sem_at = 0
-    for c in order:
-        cols = pl.ds(c * LANES, LANES)
-        here = []
-        for src, dst in (
-            (land, la.at[:, c]),
-            (thick, th.at[:, c]),
-            (temp, q.at[0:levels, c, PAD:PAD + rows]),
-            (salt, q.at[levels:2 * levels, c, PAD:PAD + rows]),
-            (uvel, q.at[2 * levels:3 * levels, c, PAD:PAD + rows]),
-            (vvel, q.at[3 * levels:4 * levels, c, PAD:PAD + rows]),
-        ):
-            here.append(pltpu.make_async_copy(src.at[:, :, cols], dst, in_sem.at[sem_at]))
-            sem_at += 1
-        for src, dst in (
-            (east_width, q.at[fa, c, PAD:PAD + rows]),
-            (north_width, q.at[fb, c, PAD:PAD + rows]),
-            (coriolis, cor.at[c]),
-        ):
-            here.append(pltpu.make_async_copy(src.at[:, cols], dst, in_sem.at[sem_at]))
-            sem_at += 1
-        for copy in here:
-            copy.start()
-        loads[c] = here
+        for i, src in enumerate((temp, salt, uvel, vvel)):
+            edge_loads.append(begin(
+                src.at[:, lo:lo + 8], edge.at[side, i * levels:(i + 1) * levels], edge_sem.at[side, i]
+            ))
+        for i, src in enumerate((east_width, north_width)):
+            edge_loads.append(begin(src.at[lo:lo + 8], edge.at[side, fa + i], edge_sem.at[side, 4 + i]))
+    for c in range(1, nc - 1):
+        begin_tile(c)
+    late = begin(coriolis, cor, whole_sem.at[2])
 
     lane, to_e, to_w = edge_lanes()
     sub = lax.broadcasted_iota(jnp.int32, (8, LANES), 0)
@@ -142,56 +132,11 @@
         for copy in loads[c]:
             copy.wait()
         for l in range(levels):
-            q[4 * levels + l, c, PAD:PAD + rows, :] = la[l, c].astype(jnp.float32) * th[l, c]
-
-    for copy in edge_loads:
+            cols = slice(c * LANES, (c + 1) * LANES)
+            q[4 * levels + l, c, PAD:PAD + rows, :] = la[l, :, cols].astype(jnp.float32) * th[l, :, cols]
+
+    for copy in whole:
         copy.wait()
-    flip = jnp.where(top, -1.0, 1.0).astype(jnp.float32)
-    for side in range(2):
-        for l in range(levels):
-            f = 4 * levels + l
-            edge[side, f] = edge_land[side, l].astype(jnp.float32) * edge[side, f]
-    for f in range(nf):
-        for c in range(nc):
-            cols = slice(c * LANES, (c + 1) * LANES)
-            row_pack[0, c, 2 * f:2 * f + 2, :] = edge[0, f, 0:2, cols]
-            near = edge[1, f, 6:7, cols]
-            far = jnp.where(top, edge[1, f, 5:6, cols], edge[1, f, 7:8, cols])
-            if 2 * levels <= f < 4 * levels:
-                near, far = near * flip, far * flip
-            row_pack[1, c, 2 * f:2 * f + 1, :] = near
-            row_pack[1, c, 2 * f + 1:2 * f + 2, :] = far
-
-    @pl.when(top)
-    def _():
-        i0 = lax.broadcasted_iota(jnp.int32, (LANES, LANES), 0)
-        i1 = lax.broadcasted_iota(jnp.int32, (LANES, LANES), 1)
-        mirror = (i0 + i1 == LANES - 1).astype(jnp.float32)
-        turned = [
-            jnp.dot(row_pack[1, c, 0:2 * nf, :], mirror, precision=lax.Precision.HIGHEST,
-                    preferred_element_type=jnp.float32)
-            for c in range(nc)
-        ]
-        for c in range(nc):
-            row_pack[1, nc - 1 - c, 0:2 * nf, :] = turned[c]
-
-    partners = 3 + e_far.astype(jnp.int32) + w_far.astype(jnp.int32) + 3 * south.astype(jnp.int32)
-    pl.semaphore_wait(barrier, partners)
-
-    def send(src, dst, s_sem, r_sem, where):
-        return pltpu.make_async_remote_copy(
-            src_ref=src, dst_ref=dst, send_sem=s_sem, recv_sem=r_sem,
-            device_id={"lat": where[0], "lon": where[1]}, device_id_type=pl.DeviceIdType.MESH,
-        )
-
-    slot = jnp.where(top, 1, 0)
-    to_north = send(row_pack.at[1], row_recv.at[slot], row_send.at[1], row_sem.at[slot], north)
-    to_south = send(row_pack.at[0], row_recv.at[1], row_send.at[0], row_sem.at[1], (lat_s, lon))
-    to_north.start()
-
-    @pl.when(south)
-    def _():
-        to_south.start()
 
     finish_load(0)
     finish_load(nc - 1)
@@ -215,6 +160,15 @@
         y = jnp.where(sub == 0, pltpu.roll(y, 2, 0), pltpu.roll(y, 4, 0))
         corner_pack[side] = jnp.where(top, y, x)
 
+    partners = 3 + e_far.astype(jnp.int32) + w_far.astype(jnp.int32) + 3 * south.astype(jnp.int32)
+    pl.semaphore_wait(barrier, partners)
+
+    def send(src, dst, s_sem, r_sem, where):
+        return pltpu.make_async_remote_copy(
+            src_ref=src, dst_ref=dst, send_sem=s_sem, recv_sem=r_sem,
+            device_id={"lat": where[0], "lon": where[1]}, device_id_type=pl.DeviceIdType.MESH,
+        )
+
     to_east = send(col_pack.at[1], col_recv.at[1, 1:nb + 1], col_send.at[1], col_sem.at[1, 1], east)
     to_west = send(col_pack.at[0], col_recv.at[0, 1:nb + 1], col_send.at[0], col_sem.at[0, 1], west)
     e_side = jnp.where(top, 0, 1)
@@ -240,6 +194,47 @@
     @pl.when(w_far)
     def _():
         to_nw.start()
+
+    for copy in edge_loads:
+        copy.wait()
+    flip = jnp.where(top, -1.0, 1.0).astype(jnp.float32)
+    for side in range(2):
+        for l in range(levels):
+            f = 4 * levels + l
+            lo = (rows - 8) * side
+            edge[side, f] = la[l, lo:lo + 8].astype(jnp.float32) * th[l, lo:lo + 8]
+    for f in range(nf):
+        for c in range(nc):
+            cols = slice(c * LANES, (c + 1) * LANES)
+            row_pack[0, c, 2 * f:2 * f + 2, :] = edge[0, f, 0:2, cols]
+            near = edge[1, f, 6:7, cols]
+            far = jnp.where(top, edge[1, f, 5:6, cols], edge[1, f, 7:8, cols])
+            if 2 * levels <= f < 4 * levels:
+                near, far = near * flip, far * flip
+            row_pack[1, c, 2 * f:2 * f + 1, :] = near
+            row_pack[1, c, 2 * f + 1:2 * f + 2, :] = far
+
+    @pl.when(top)
+    def _():
+        i0 = lax.broadcasted_iota(jnp.int32, (LANES, LANES), 0)
+        i1 = lax.broadcasted_iota(jnp.int32, (LANES, LANES), 1)
+        mirror = (i0 + i1 == LANES - 1).astype(jnp.float32)
+        turned = [
+            jnp.dot(row_pack[1, c, 0:2 * nf, :], mirror, precision=lax.Precision.HIGHEST,
+                    preferred_element_type=jnp.float32)
+            for c in range(nc)
+        ]
+        for c in range(nc):
+            row_pack[1, nc - 1 - c, 0:2 * nf, :] = turned[c]
+
+    slot = jnp.where(top, 1, 0)
+    to_north = send(row_pack.at[1], row_recv.at[slot], row_send.at[1], row_sem.at[slot], north)
+    to_south = send(row_pack.at[0], row_recv.at[1], row_send.at[0], row_sem.at[1], (lat_s, lon))
+    to_north.start()
+
+    @pl.when(south)
+    def _():
+        to_south.start()
 
     for c in range(1, nc - 1):
         finish_load(c)
@@ -313,14 +308,6 @@
             x = pltpu.roll(e, LANES - 2 * f, 1) if f else e
             q[f, nc, pl.ds(s, 8), :] = jnp.where(lane < 64, x, pltpu.roll(w, LANES - 2 - 2 * f, 1))
 
-    def row_a(s, tiles):
-        for c in tiles:
-            pass_a(s, c)
-
-    def row_b(j):
-        for c in range(nc):
-            pass_b(j, c)
-
     loop(nb - 1, lambda k: row_a(PAD - 1 + 8 * (1 + k), range(1, nc - 1)))
     to_east.wait_recv()
     to_west.wait_recv()
@@ -365,6 +352,7 @@
 
     loop(2, lambda i: row_a(PAD - 1 + (rows - 6) * i, range(ring)))
 
+    late.wait()
     to_east.wait_send()
     to_west.wait_send()
     to_north.wait_send()
@@ -402,11 +390,11 @@
         cols = slice(c * LANES, (c + 1) * LANES)
         ga = (0.5 * time_step) * inverse(q[fa, c, r0, :])
         gb = (0.5 * time_step) * inverse(q[fb, c, r0, :])
-        rot = time_step * cor[c, ro, :]
+        rot = time_step * cor[ro, cols]
         for l in range(levels):
             ce, cw = cf[l, c, r0, :], cf[levels + l, c, r0, :]
             cn, cs = cf[2 * levels + l, c, r0, :], cf[3 * levels + l, c, r0, :]
-            wet = la[l, c, ro, :].astype(jnp.float32)
+            wet = la[l, ro, cols].astype(jnp.float32)
 
             def drag(v):
                 f = v * levels + l
@@ -426,25 +414,27 @@
 
     outs = (temp_out, salt_out, uvel_out, vvel_out)
 
+    def store(j):
+        t = pl.multiple_of(8 * j, 8)
+        return [
+            pltpu.make_async_copy(
+                ob.at[i * levels:(i + 1) * levels, pl.ds(t, 8)], dst.at[:, pl.ds(t, 8)], out_sem.at[j, i]
+            )
+            for i, dst in enumerate(outs)
+        ]
+
     def row_b(j):
         for c in range(nc):
             pass_b(j, c)
-
-    stores = []
-    size = rows // PARTS
-    for part in range(PARTS):
-        lo = part * size
-        loop(size // 8, lambda j: row_b(lo // 8 + j))
-        for i, dst in enumerate(outs):
-            copy = pltpu.make_async_copy(
-                ob.at[i * levels:(i + 1) * levels, lo:lo + size],
-                dst.at[:, lo:lo + size],
-                out_sem.at[part, i],
-            )
+        for copy in store(j):
             copy.start()
-            stores.append(copy)
-    for copy in stores:
-        copy.wait()
+
+    def settle(j):
+        for copy in store(j):
+            copy.wait()
+
+    loop(nb, row_b)
+    loop(nb, settle)
 
 
 def shards(n_lat, n_lon, *args):
@@ -465,8 +455,8 @@
         functools.partial(first_kernel, n_lat, n_lon),
         out_shape=(
             plane(nf),
-            pltpu.VMEM((levels, nc, rows, LANES), jnp.int32),
-            pltpu.VMEM((nc, rows, LANES), f32),
+            pltpu.VMEM((levels, rows, width), jnp.int32),
+            pltpu.VMEM((rows, width), f32),
             plane(4 * levels),
             plane(4 * levels),
             plane(levels),
@@ -475,16 +465,16 @@
         in_specs=[far] * 9,
         out_specs=(held,) * 7,
         scratch_shapes=[
-            pltpu.VMEM((levels, nc, rows, LANES), f32),
+            pltpu.VMEM((levels, rows, width), f32),
             pltpu.VMEM((2, nf, 8, width), f32),
-            pltpu.VMEM((2, levels, 8, width), jnp.int32),
             pltpu.VMEM((2, nc, row_slots, LANES), f32),
             pltpu.VMEM((2, nc, row_slots, LANES), f32),
             pltpu.VMEM((2, nb, 8, LANES), f32),
             pltpu.VMEM((2, 8, LANES), f32),
             pltpu.VMEM((2, nb + 2, 8, LANES), f32),
-            dma((16,)),
-            dma((9 * nc,)),
+            dma((3,)),
+            dma((2, 6)),
+            dma((nc, 6)),
             dma((2,)),
             dma((2,)),
             dma((2,)),
@@ -502,7 +492,7 @@
         out_specs=(far,) * 4,
         scratch_shapes=[
             pltpu.VMEM((4 * levels, rows, width), f32),
-            dma((PARTS, 4)),
+            dma((nb, 4)),
         ],
         compiler_params=pltpu.CompilerParams(vmem_limit_bytes=LIMIT * 1024 * 1024),
     )(*middle)

time: 18 us -> 16.8 us (0.933)
  the two profiles are of different devices: /device:TPU:25 before, /device:TPU:0 now
where the time goes in v4:
time: 16.8 us; the launch traced here: 16.7 us
  Pallas kernels  16 us (95%)
  between operations  0.64 us (4%)
    pallas_call x1, Pallas kernels, shards(): pl.pallas_call(functools.partial(first_kernel, n_lat, n_lon), out_shape=(...  11.8 us
    pallas_call x1, Pallas kernels, shards(): pl.pallas_call(second_kernel, out_shape=tuple((jax.ShapeDtypeStruct((leve...  4.19 us

profile of v4, /device:TPU:0, one launch (start us, length us, event | category | flops | bytes accessed | tf_op | source)
XLA Modules:
  0.0 16.7 jit_solution(17482508047047379602)
XLA Ops:
  0.6 11.8 %shard_map.120 = (f32[22,7,80,128]{3,2,1,0:T(8,128)S(1)}, s32[4,64,768]{2,1,0:T(8,128)S(1)}, f32[64,768]{1,0:T(8,128)S(1)}, f32[16,7,80,128]{3,2,1,0:T(8,128)S(1...) custom-call(f32[4,64,768]{2,1,0:T(8,128)} %temp.1, ...), custom_call_target="tpu_custom_call" | custom-call | tf_op jit(solution)/shard_map/pallas_call | solution.py:454
  12.5 4.2 %shard_map.121 = (f32[4,64,768]{2,1,0:T(8,128)}, f32[4,64,768]{2,1,0:T(8,128)}, f32[4,64,768]{2,1,0:T(8,128)}, f32[4,64,768]{2,1,0:T(8,128)}) custom-call(f32[22,7,80,128]{3,2,1,0:T(8,128)S(1)} %get-tuple-element.11.q, s32[4,64,768]{2,1,0:T(8,128)S(1)} %get-tuple-element.12.la, f32[64,768]{1,0:T(8,128)S(1)} %get-tuple-element.13.cor, ...), custom_call_target="tpu_custom_call" | custom-call | tf_op jit(solution)/shard_map/pallas_call | solution.py:488

commit v5 on v4

--- a/solution.py
+++ b/solution.py
@@ -140,25 +140,29 @@
 
     finish_load(0)
     finish_load(nc - 1)
-    lane_r = lax.broadcasted_iota(jnp.int32, (rows, LANES), 1)
-    head = jnp.zeros((rows, LANES), jnp.float32)
-    tail = jnp.zeros((rows, LANES), jnp.float32)
-    for f in range(nf):
-        mine = lane_r // 2 == f
-        a0 = q[f, 0, PAD:PAD + rows, :]
-        a1 = q[f, nc - 1, PAD:PAD + rows, :]
-        head = jnp.where(mine, pltpu.roll(a0, 2 * f, 1) if f else a0, head)
-        tail = jnp.where(mine, pltpu.roll(a1, 2 * f + 2, 1), tail)
-    col_pack[0] = head.reshape(nb, 8, LANES)
-    col_pack[1] = tail.reshape(nb, 8, LANES)
+    own = [jnp.logical_and(lane >= 4 * f, lane < 4 * f + 4) for f in range(nf)]
+
+    def pack_cols(k):
+        r = pl.ds(pl.multiple_of(PAD + 8 * k, 8), 8)
+        block = jnp.zeros((8, LANES), jnp.float32)
+        for f in range(nf):
+            ends = jnp.where(lane < LANES // 2, q[f, 0, r, :], q[f, nc - 1, r, :])
+            block = jnp.where(own[f], pltpu.roll(ends, 4 * f + 2, 1), block)
+        col_pack[k] = block
+
+    loop(nb, pack_cols)
     sign_lane = jnp.where(
-        jnp.logical_and(lane >= 4 * levels, lane < 8 * levels), -1.0, 1.0
+        jnp.logical_and(lane >= 8 * levels, lane < 16 * levels), -1.0, 1.0
     ).astype(jnp.float32)
-    for side, block in ((0, head), (1, tail)):
-        x = block[rows - 8:rows, :]
-        y = jnp.where(lane % 2 == 0, pltpu.roll(x, LANES - 1, 1), pltpu.roll(x, 1, 1)) * sign_lane
-        y = jnp.where(sub == 0, pltpu.roll(y, 2, 0), pltpu.roll(y, 4, 0))
-        corner_pack[side] = jnp.where(top, y, x)
+    x = col_pack[nb - 1]
+    place = lane % 4
+    y = jnp.where(
+        place < 2,
+        jnp.where(place == 0, pltpu.roll(x, LANES - 3, 1), pltpu.roll(x, LANES - 1, 1)),
+        jnp.where(place == 2, pltpu.roll(x, 1, 1), pltpu.roll(x, 3, 1)),
+    ) * sign_lane
+    y = jnp.where(sub == 0, pltpu.roll(y, 2, 0), pltpu.roll(y, 4, 0))
+    corner_pack[...] = jnp.where(top, y, x)
 
     partners = 3 + e_far.astype(jnp.int32) + w_far.astype(jnp.int32) + 3 * south.astype(jnp.int32)
     pl.semaphore_wait(barrier, partners)
@@ -169,16 +173,16 @@
             device_id={"lat": where[0], "lon": where[1]}, device_id_type=pl.DeviceIdType.MESH,
         )
 
-    to_east = send(col_pack.at[1], col_recv.at[1, 1:nb + 1], col_send.at[1], col_sem.at[1, 1], east)
-    to_west = send(col_pack.at[0], col_recv.at[0, 1:nb + 1], col_send.at[0], col_sem.at[0, 1], west)
+    to_east = send(col_pack, col_recv.at[1, 1:nb + 1], col_send.at[1], col_sem.at[1, 1], east)
+    to_west = send(col_pack, col_recv.at[0, 1:nb + 1], col_send.at[0], col_sem.at[0, 1], west)
     e_side = jnp.where(top, 0, 1)
     w_side = jnp.where(top, 1, 0)
     blk = jnp.where(top, nb + 1, 0)
     which = jnp.where(top, 2, 0)
-    to_ne = send(corner_pack.at[1], col_recv.at[e_side, blk], corner_send.at[0], col_sem.at[e_side, which], north_e)
-    to_nw = send(corner_pack.at[0], col_recv.at[w_side, blk], corner_send.at[1], col_sem.at[w_side, which], north_w)
-    to_se = send(col_pack.at[1, 0], col_recv.at[1, nb + 1], corner_send.at[2], col_sem.at[1, 2], (lat_s, east_lon))
-    to_sw = send(col_pack.at[0, 0], col_recv.at[0, nb + 1], corner_send.at[3], col_sem.at[0, 2], (lat_s, west_lon))
+    to_ne = send(corner_pack, col_recv.at[e_side, blk], corner_send.at[0], col_sem.at[e_side, which], north_e)
+    to_nw = send(corner_pack, col_recv.at[w_side, blk], corner_send.at[1], col_sem.at[w_side, which], north_w)
+    to_se = send(col_pack.at[0], col_recv.at[1, nb + 1], corner_send.at[2], col_sem.at[1, 2], (lat_s, east_lon))
+    to_sw = send(col_pack.at[0], col_recv.at[0, nb + 1], corner_send.at[3], col_sem.at[0, 2], (lat_s, west_lon))
     to_east.start()
     to_west.start()
 
@@ -303,10 +307,9 @@
 
     def unpack_cols(block):
         s = pl.multiple_of(8 * block, 8)
-        e, w = col_recv[0, block], col_recv[1, block]
+        both = jnp.where(lane % 4 < 2, col_recv[1, block], col_recv[0, block])
         for f in range(nf):
-            x = pltpu.roll(e, LANES - 2 * f, 1) if f else e
-            q[f, nc, pl.ds(s, 8), :] = jnp.where(lane < 64, x, pltpu.roll(w, LANES - 2 - 2 * f, 1))
+            q[f, nc, pl.ds(s, 8), :] = pltpu.roll(both, LANES - 2 - 4 * f, 1)
 
     loop(nb - 1, lambda k: row_a(PAD - 1 + 8 * (1 + k), range(1, nc - 1)))
     to_east.wait_recv()
@@ -317,8 +320,8 @@
     @pl.when(south)
     def _():
         send(row_pack.at[1], row_recv.at[0], row_send.at[1], row_sem.at[0], north).wait_recv()
-        send(corner_pack.at[1], col_recv.at[1, 0], corner_send.at[0], col_sem.at[1, 0], east).wait_recv()
-        send(corner_pack.at[0], col_recv.at[0, 0], corner_send.at[1], col_sem.at[0, 0], west).wait_recv()
+        send(corner_pack, col_recv.at[1, 0], corner_send.at[0], col_sem.at[1, 0], east).wait_recv()
+        send(corner_pack, col_recv.at[0, 0], corner_send.at[1], col_sem.at[0, 0], west).wait_recv()
         for f in range(nf):
             q[f, 0:nc, PAD - 2:PAD, :] = row_recv[0, :, 2 * f:2 * f + 2, :]
         unpack_cols(0)
@@ -332,19 +335,19 @@
 
     @pl.when(e_far)
     def _():
-        send(corner_pack.at[1], col_recv.at[0, nb + 1], corner_send.at[0], col_sem.at[0, 2], east).wait_recv()
+        send(corner_pack, col_recv.at[0, nb + 1], corner_send.at[0], col_sem.at[0, 2], east).wait_recv()
 
     @pl.when(e_self)
     def _():
-        col_recv[0, nb + 1] = corner_pack[1]
+        col_recv[0, nb + 1] = corner_pack[...]
 
     @pl.when(w_far)
     def _():
-        send(corner_pack.at[0], col_recv.at[1, nb + 1], corner_send.at[1], col_sem.at[1, 2], west).wait_recv()
+        send(corner_pack, col_recv.at[1, nb + 1], corner_send.at[1], col_sem.at[1, 2], west).wait_recv()
 
     @pl.when(w_self)
     def _():
-        col_recv[1, nb + 1] = corner_pack[0]
+        col_recv[1, nb + 1] = corner_pack[...]
 
     for f in range(nf):
         q[f, 0:nc, PAD + rows:PAD + rows + 2, :] = row_recv[1, :, 2 * f:2 * f + 2, :]
@@ -469,8 +472,8 @@
             pltpu.VMEM((2, nf, 8, width), f32),
             pltpu.VMEM((2, nc, row_slots, LANES), f32),
             pltpu.VMEM((2, nc, row_slots, LANES), f32),
-            pltpu.VMEM((2, nb, 8, LANES), f32),
-            pltpu.VMEM((2, 8, LANES), f32),
+            pltpu.VMEM((nb, 8, LANES), f32),
+            pltpu.VMEM((8, LANES), f32),
             pltpu.VMEM((2, nb + 2, 8, LANES), f32),
             dma((3,)),
             dma((2, 6)),

time: 16.8 us -> 17 us (1.012)
  no operation moved by 1% of the time
where the time goes in v5:
time: 17 us; the launch traced here: 16.8 us
  Pallas kernels  16.1 us (95%)
  between operations  0.64 us (4%)
    pallas_call x1, Pallas kernels, shards(): pl.pallas_call(functools.partial(first_kernel, n_lat, n_lon), out_shape=(...  11.9 us
    pallas_call x1, Pallas kernels, shards(): pl.pallas_call(second_kernel, out_shape=tuple((jax.ShapeDtypeStruct((leve...  4.19 us

profile of v5, /device:TPU:0, one launch (start us, length us, event | category | flops | bytes accessed | tf_op | source)
XLA Modules:
  0.0 16.8 jit_solution(11949036035598712568)
XLA Ops:
  0.6 11.9 %shard_map.120 = (f32[22,7,80,128]{3,2,1,0:T(8,128)S(1)}, s32[4,64,768]{2,1,0:T(8,128)S(1)}, f32[64,768]{1,0:T(8,128)S(1)}, f32[16,7,80,128]{3,2,1,0:T(8,128)S(1...) custom-call(f32[4,64,768]{2,1,0:T(8,128)} %temp.1, ...), custom_call_target="tpu_custom_call" | custom-call | tf_op jit(solution)/shard_map/pallas_call | solution.py:457
  12.6 4.2 %shard_map.121 = (f32[4,64,768]{2,1,0:T(8,128)}, f32[4,64,768]{2,1,0:T(8,128)}, f32[4,64,768]{2,1,0:T(8,128)}, f32[4,64,768]{2,1,0:T(8,128)}) custom-call(f32[22,7,80,128]{3,2,1,0:T(8,128)S(1)} %get-tuple-element.11.q, s32[4,64,768]{2,1,0:T(8,128)S(1)} %get-tuple-element.12.la, f32[64,768]{1,0:T(8,128)S(1)} %get-tuple-element.13.cor, ...), custom_call_target="tpu_custom_call" | custom-call | tf_op jit(solution)/shard_map/pallas_call | solution.py:491

commit v6 on v5

--- a/solution.py
+++ b/solution.py
@@ -207,10 +207,21 @@
             f = 4 * levels + l
             lo = (rows - 8) * side
             edge[side, f] = la[l, lo:lo + 8].astype(jnp.float32) * th[l, lo:lo + 8]
+    slot = jnp.where(top, 1, 0)
+    to_north = send(row_pack.at[1], row_recv.at[slot], row_send.at[1], row_sem.at[slot], north)
+    to_south = send(row_pack.at[0], row_recv.at[1], row_send.at[0], row_sem.at[1], (lat_s, lon))
     for f in range(nf):
         for c in range(nc):
             cols = slice(c * LANES, (c + 1) * LANES)
             row_pack[0, c, 2 * f:2 * f + 2, :] = edge[0, f, 0:2, cols]
+
+    @pl.when(south)
+    def _():
+        to_south.start()
+
+    for f in range(nf):
+        for c in range(nc):
+            cols = slice(c * LANES, (c + 1) * LANES)
             near = edge[1, f, 6:7, cols]
             far = jnp.where(top, edge[1, f, 5:6, cols], edge[1, f, 7:8, cols])
             if 2 * levels <= f < 4 * levels:
@@ -231,14 +242,7 @@
         for c in range(nc):
             row_pack[1, nc - 1 - c, 0:2 * nf, :] = turned[c]
 
-    slot = jnp.where(top, 1, 0)
-    to_north = send(row_pack.at[1], row_recv.at[slot], row_send.at[1], row_sem.at[slot], north)
-    to_south = send(row_pack.at[0], row_recv.at[1], row_send.at[0], row_sem.at[1], (lat_s, lon))
     to_north.start()
-
-    @pl.when(south)
-    def _():
-        to_south.start()
 
     for c in range(1, nc - 1):
         finish_load(c)

time: 17 us -> 17 us (level)
  no operation moved by 1% of the time
where the time goes in v6:
time: 17 us; the launch traced here: 16.8 us
  Pallas kernels  16.1 us (95%)
  between operations  0.64 us (4%)
    pallas_call x1, Pallas kernels, shards(): pl.pallas_call(functools.partial(first_kernel, n_lat, n_lon), out_shape=(...  11.9 us
    pallas_call x1, Pallas kernels, shards(): pl.pallas_call(second_kernel, out_shape=tuple((jax.ShapeDtypeStruct((leve...  4.19 us

profile of v6, /device:TPU:0, one launch (start us, length us, event | category | flops | bytes accessed | tf_op | source)
XLA Modules:
  0.0 16.8 jit_solution(6491588056800121125)
XLA Ops:
  0.6 11.9 %shard_map.120 = (f32[22,7,80,128]{3,2,1,0:T(8,128)S(1)}, s32[4,64,768]{2,1,0:T(8,128)S(1)}, f32[64,768]{1,0:T(8,128)S(1)}, f32[16,7,80,128]{3,2,1,0:T(8,128)S(1...) custom-call(f32[4,64,768]{2,1,0:T(8,128)} %temp.1, ...), custom_call_target="tpu_custom_call" | custom-call | tf_op jit(solution)/shard_map/pallas_call | solution.py:461
  12.6 4.2 %shard_map.121 = (f32[4,64,768]{2,1,0:T(8,128)}, f32[4,64,768]{2,1,0:T(8,128)}, f32[4,64,768]{2,1,0:T(8,128)}, f32[4,64,768]{2,1,0:T(8,128)}) custom-call(f32[22,7,80,128]{3,2,1,0:T(8,128)S(1)} %get-tuple-element.11.q, s32[4,64,768]{2,1,0:T(8,128)S(1)} %get-tuple-element.12.la, f32[64,768]{1,0:T(8,128)S(1)} %get-tuple-element.13.cor, ...), custom_call_target="tpu_custom_call" | custom-call | tf_op jit(solution)/shard_map/pallas_call | solution.py:495
